TPU v7x, 32 devices: a whole 2x2x4 slice. The times are simulated.
32 devices in a mesh: parts: 2 (over x), xfer: 16 (over z, y, core).
Axes of the slice: x: 2, y: 2, z: 4, core: 2. Of those that a mesh axis runs over, the one named last changes fastest.
Arguments:
- hidden_in: bfloat16 [64, 2, 8192], P(('parts', 'xfer')), parts along dimension 0, may hold values from -6 to 6
- latent_cache: bfloat16 [32, 16384, 512], P('parts', 'xfer'), parts along dimension 0, may hold values from -1600 to 1600
- lengths: int32 [32], P('parts'), parts along dimension 0, may hold values from 1 to 16384, 131072 in all
- placement: int32 [32], P('parts'), parts along dimension 0, may hold values from 0 to 15, each once
- w_query: bfloat16 [8192, 8192], P(None, 'xfer'), may hold values from -0.0625 to 0.0625
- w_down: bfloat16 [8192, 512], P(None, 'xfer'), may hold values from -0.0625 to 0.0625
- up_key: bfloat16 [256, 1024], replicated, may hold values from -0.5 to 0.5
- up_value: bfloat16 [256, 1024], replicated, may hold values from -0.375 to 0.375
- w_out: bfloat16 [8192, 8192], P('xfer'), may hold values from -0.0625 to 0.0625
Outputs:
- attended: bfloat16 [64, 2, 8192], P(('parts', 'xfer')), parts along dimension 0
There are 2 independent parts, one for each index of `parts`. A program takes and returns all parts, laid end to end along the dimension named above; an argument that names none is the same for every part. Nothing has to cross between parts.
Inputs may be any that keep to these rules, and one draw needn't show every extreme that they name: `lengths`: prompt length of each request; some request has exactly 16384 positions. Each request appears once; request placement[j] is decoded by devices j * 1 to (j + 1) - 1, each holding 2 of its samples in order.
All inputs are finite; a program needn't handle non-finite values.
Results may differ from a plain program's by a relative error of at most 0.012.
The roundings to bfloat16 on the way count: a program that leaves them out, or rounds other values in their place, can miss the bound.
Values may be sent and summed in bfloat16 or wider, within the bound.
A program may use at most 192 MiB of HBM per device.

v0:
```python
import jax
import jax.numpy as jnp
from jax import lax
from jax.sharding import PartitionSpec as P

HEADS = 64
KVH = 8
HD = 128
R = 16


def expand(up, rank):
    return jnp.repeat(up.reshape(rank, KVH, HD), HEADS // KVH, axis=1).astype(jnp.float32)


def decode_attention(queries, own, cache, seen, up_key, up_value):
    highest = lax.Precision.HIGHEST
    rank = up_key.shape[0]
    longest = cache.shape[1]
    key_up = expand(up_key, rank)
    value_up = expand(up_value, rank)
    scale = HD ** (-0.5)
    absorbed = jnp.einsum(
        "isthd,rhd->isthr", queries.astype(jnp.float32), key_up, precision=highest
    )
    far = (
        jnp.einsum(
            "isthr,ilr->isthl", absorbed, cache[..., :rank].astype(jnp.float32), precision=highest
        )
        * scale
    )
    positions = jnp.arange(longest, dtype=jnp.int32)
    valid = positions[None, :] < seen[:, None]
    far = jnp.where(valid[:, None, None, None, :], far, -1e30)
    near = (
        jnp.einsum(
            "isthr,isur->isthu", absorbed, own[..., :rank].astype(jnp.float32), precision=highest
        )
        * scale
    )
    steps_mask = jnp.tril(jnp.ones((2, 2), dtype=bool))
    near = jnp.where(steps_mask[None, None, :, None, :], near, -1e30)
    top = jnp.maximum(jnp.max(far, -1), jnp.max(near, -1))
    far_w = jnp.exp(far - top[..., None])
    near_w = jnp.exp(near - top[..., None])
    total = jnp.sum(far_w, -1) + jnp.sum(near_w, -1)
    far_b = far_w.astype(jnp.bfloat16)
    near_b = near_w.astype(jnp.bfloat16)
    latent_out = jnp.einsum(
        "isthl,ilr->isthr", far_b, cache[..., rank:], preferred_element_type=jnp.float32
    )
    latent_out = latent_out + jnp.einsum(
        "isthu,isur->isthr", near_b, own[..., rank:], preferred_element_type=jnp.float32
    )
    latent_out = latent_out / total[..., None]
    return jnp.einsum("isthr,rhd->isthd", latent_out, value_up, precision=highest).astype(
        jnp.bfloat16
    )


def local(hidden_in, latent_cache, lengths, placement, w_query, w_down, up_key, up_value, w_out):
    ndevs = lax.axis_size("xfer")
    mine = lax.axis_index("xfer")
    rank = up_key.shape[0]
    query_cols = w_query.shape[1]
    slot_rows = hidden_in.shape[0]
    group = ndevs // R
    samples = slot_rows * group
    piece = lax.all_gather(hidden_in, "xfer", axis=0, tiled=True)
    query = jnp.einsum("rtd,dk->rtk", piece, w_query, preferred_element_type=jnp.float32).astype(
        jnp.bfloat16
    )
    fresh = jnp.einsum("rtd,dk->rtk", piece, w_down, preferred_element_type=jnp.float32).astype(
        jnp.bfloat16
    )
    projected = jnp.concatenate([query, fresh], axis=2)
    offsets = jnp.arange(samples, dtype=jnp.int32)
    row_index = (placement[:, None] * samples + offsets[None, :]).reshape(-1)
    projected = projected[row_index]
    query_part = projected[..., :query_cols]
    fresh_part = projected[..., query_cols:]
    query_blocks = query_part.reshape(ndevs, slot_rows, 2, query_cols)
    fresh_blocks = fresh_part.reshape(ndevs, slot_rows, 2, -1)
    queries, own = (
        lax.all_to_all(query_blocks, "xfer", split_axis=0, concat_axis=3, tiled=True),
        lax.all_to_all(fresh_blocks, "xfer", split_axis=0, concat_axis=3, tiled=True),
    )
    queries = queries.reshape(1, slot_rows, 2, HEADS, HD)
    target_requests = placement[jnp.arange(ndevs, dtype=jnp.int32) // group]
    outgoing = latent_cache[target_requests][:, None]
    cache = lax.all_to_all(outgoing, "xfer", split_axis=0, concat_axis=2, tiled=True)
    cache = cache.reshape(1, -1, 2 * rank)
    my_request = lax.dynamic_slice_in_dim(placement, mine // group, 1)
    seen = lengths[my_request]
    head_out = decode_attention(queries, own, cache, seen, up_key, up_value)
    head_out = head_out.reshape(slot_rows, 2, HEADS * HD)
    gathered = lax.all_to_all(head_out, "xfer", split_axis=2, concat_axis=0, tiled=True)
    piece = gathered
    summed = lax.psum_scatter(
        jnp.einsum("rtk,kd->rtd", piece, w_out, preferred_element_type=jnp.float32),
        "xfer",
        scatter_dimension=0,
        tiled=True,
    )
    attended = summed.astype(jnp.bfloat16)
    return attended


def solution(mesh):
    placed = (
        P(("parts", "xfer"), None, None),
        P("parts", "xfer", None),
        P("parts"),
        P("parts"),
        P(None, "xfer"),
        P(None, "xfer"),
        P(),
        P(),
        P("xfer", None),
    )
    return jax.shard_map(
        local,
        mesh=mesh,
        in_specs=placed,
        out_specs=P(("parts", "xfer"), None, None),
        check_vma=False,
    )
```

profile of v0, /device:TPU:0, one launch (start us, length us, event | category | flops | bytes accessed | tf_op | source)
XLA Modules:
  0.0 626.4 jit_solution(2184652916584348774)
XLA Ops:
  6.5 0.0 copy-start
  6.5 0.0 copy-start.2
  6.5 0.0 copy-start.5
  6.5 0.0 all-gather.2.cloned.1.call-start
  6.5 0.7 all-gather.2.cloned.1.call-update
  7.3 0.7 broadcast_multiply_fusion
  7.9 0.1 iota_add_fusion
  8.0 0.1 add.78
  8.1 42.1 %all-gather.2.cloned.1.call-done = bf16[32,2,8192]{2,1,0:T(2,128)(2,1)} async-done(((bf16[2,2,8192]{2,1,0:T(2,128)(2,1)}), bf16[32,2,8192]{2,1,0:T(2,128)(2,1)}) %all-gather.2.cloned.1.call-update) | async-done | bytes 1048592 | tf_op jit(solution)/shard_map/all_gather | solution.py:69
  50.2 0.0 copy-start.3
  50.2 5.4 fusion.11
  55.6 0.0 copy-done.5
  55.7 0.0 copy-done.3
  55.7 0.8 convolution_convert_fusion.1
  56.5 0.1 copy.31
  56.6 0.7 gather_fusion
  57.3 0.6 slice.37
  58.0 3.6 all-to-all-start.2
  61.6 0.0 copy-done.2
  61.6 0.7 gather_fusion.1
  62.3 0.7 slice.35
  63.0 5.1 all-to-all-done.2
  68.1 3.5 all-to-all-start
  71.6 13.0 %gather_fusion.2 = bf16[16,1024,512]{2,1,0:T(8,128)(2,1)} fusion(bf16[16,1024,512]{2,1,0:T(8,128)(2,1)} %param.10, s32[1024]{0:T(1024)S(1)} %pad_clamp_fusion), kind=kCustom, calls=%fused_computation.2 | custom fusion | bytes 33554496 | tf_op jit(solution)/shard_map/gather | solution.py:90
  84.6 0.0 all-to-all-done
  84.6 0.0 copy-start.6
  84.7 0.0 copy-start.4
  84.7 6.2 all-to-all-start.1
  90.8 0.6 dynamic_slice.3
  93.4 0.0 copy-done.6
  93.4 0.6 dynamic-slice.2
  94.0 0.6 iota_compare_fusion
  94.6 0.0 copy-done
  94.6 0.1 copy_bitcast_fusion.1
  94.7 0.0 copy-done.4
  94.7 0.1 copy_bitcast_fusion
  94.9 0.1 all_to_all.51
  95.0 0.1 reshape.172
  95.0 1.1 broadcast_in_dim.50
  96.1 1.2 convolution_bitcast_fusion
  97.3 0.3 fusion.30
  97.6 290.0 %all-to-all-done.1 = bf16[16,1,1024,512]{3,2,1,0:T(8,128)(2,1)} async-done(((bf16[16,1,1024,512]{3,2,1,0:T(8,128)(2,1)}), bf16[16,1,1024,512]{3,2,1,0:T(8,128)(2,1)}, u32[]{:S(2)}, u32[]{:S(2)}) %all-to-all-start.1) | async-done | bytes 16777248 | tf_op jit(solution)/shard_map/all_to_all | solution.py:91
  387.6 23.7 %fusion.29 = (f32[2,2,64]{2,1,0:T(2,128)S(1)}, f32[2,2,64,16384]{3,2,1,0:T(8,128)}) fusion(bf16[1,16384,512]{2,1,0:T(8,128)(2,1)} %bitcast.18, f32[2,2,64,256]{3,1,0,2:T(2,128)S(1)} %convolution_bitcast_fusion, pred[16384]{0:T(1024)(128)(4,1)S(1)} %iota_compare_fusion), kind=kOutput, calls=%fused_computation.53 | convolution fusion | flops 12897484800 | bytes 25445376 | tf_op jit(solution)/shard_map/isthr,ilr->isthl/dot_general | solution.py:27
  411.3 8.1 %fusion.1 = f32[2,2,64]{2,1,0:T(2,128)S(1)} fusion(f32[2,2,64,16384]{3,2,1,0:T(8,128)} %get-tuple-element.17, f32[2,2,64]{2,1,0:T(2,128)S(1)} %max.9), kind=kLoop, calls=%fused_computation.6 | loop fusion | flops 8388352 | bytes 16779264 | tf_op jit(solution)/shard_map/reduce_sum | solution.py:46
  419.4 9.8 %fusion.3 = f32[2,2,64,256]{3,2,1,0:T(8,128)S(1)} fusion(f32[2,2,64,16384]{3,2,1,0:T(8,128)} %get-tuple-element.17, bf16[1,16384,512]{2,1,0:T(8,128)(2,1)} %bitcast.18, f32[2,2,64]{2,1,0:T(2,128)S(1)} %max.9), kind=kOutput, calls=%fused_computation.8 | convolution fusion | flops 2155872256 | bytes 25428992 | tf_op jit(solution)/shard_map/isthl,ilr->isthr/dot_general | solution.py:49
  429.3 0.2 fusion.10
  429.5 0.0 copy-start.7
  429.6 1.0 broadcast_in_dim.55
  430.6 1.8 fusion.14
  432.4 6.9 %copy.51 = bf16[1,2,2,64,128]{2,1,4,3,0:T(2,128)(2,1)} copy(bf16[1,2,2,64,128]{4,2,1,3,0:T(2,128)(2,1)S(1)} %fusion.14) | data formatting | bytes 131072 | tf_op jit(solution)/shard_map/reshape | solution.py:96
  439.3 7.8 %reshape.242 = bf16[16,2,1024]{2,1,0:T(2,128)(2,1)} reshape(bf16[8192,2,2]{2,1,0:T(2,128)(2,1)} %bitcast.111) | data formatting | bytes 131072
  447.1 70.2 %all-to-all-start.3 = ((bf16[16,2,1024]{2,1,0:T(2,128)(2,1)}), bf16[16,2,1024]{2,1,0:T(2,128)(2,1)S(1)}, u32[]{:S(2)}, u32[]{:S(2)}) async-start(bf16[16,2,1024]{2,1,0:T(2,128)(2,1)} %reshape.242), calls=%async_computation.3 | async-start | bytes 131072 | tf_op jit(solution)/shard_map/all_to_all | solution.py:97
  517.3 0.0 copy-done.7
  517.3 0.7 dynamic-slice.3
  518.7 5.5 all-to-all-done.3
  524.2 10.0 %reshape.243 = bf16[8192,2,2]{2,1,0:T(2,128)(2,1)} reshape(bf16[16,2,1024]{2,1,0:T(2,128)(2,1)S(1)} %all-to-all-done.3) | data formatting | bytes 131072
  534.2 0.0 copy-start.1
  534.2 6.2 copy.52
  540.4 0.1 copy.43
  540.5 5.0 fusion.5
  545.4 72.4 %all-reduce.2 = bf16[32,2,8192]{2,0,1:T(8,128)(2,1)} all-reduce(f32[32,2,8192]{2,0,1:T(8,128)S(1)} %fusion.5), channel_id=2, replica_groups=mesh['parts'=2,'xfer'=16] {'xfer'}, use_global_device_ids=true, to_apply=%region_4.5.clone | all-reduce | flops 524288 | bytes 3145728
  617.8 1.0 dynamic-slice_convert_fusion
  618.8 0.7 copy.44
  619.5 0.0 copy-done.1
  (14 shorter events, 0.1 us)
Async XLA Ops:
  6.5 88.1 %copy-start = (bf16[256,1024]{1,0:T(8,128)(2,1)S(1)}, bf16[256,1024]{1,0:T(8,128)(2,1)}, u32[]{:S(2)}) copy-start(bf16[256,1024]{1,0:T(8,128)(2,1)} %param.15) | copy-start | bytes 1572868
  6.5 55.1 %copy-start.2 = (s32[16]{0:T(128)S(1)}, s32[16]{0:T(128)}, u32[]{:S(2)}) copy-start(s32[16]{0:T(128)} %param.12) | copy-start | bytes 196
  6.5 49.1 %copy-start.5 = (bf16[8192,32]{0,1:T(8,128)(2,1)S(1)}, bf16[8192,32]{0,1:T(8,128)(2,1)}, u32[]{:S(2)}) copy-start(bf16[8192,32]{0,1:T(8,128)(2,1)} %param.14) | copy-start | bytes 1572868
  6.5 43.7 %all-gather.2.cloned.1.call-start = ((), (), s32[]{:S(2)}) async-start(), calls=%async_computation.4 | async-start | bytes 1114112 | tf_op jit(solution)/shard_map/all_gather | solution.py:69
  50.2 5.5 copy-start.3
  58.0 10.1 %all-to-all-start.2 = ((bf16[16,2,2,32]{3,2,1,0:T(2,128)(2,1)}), bf16[16,2,2,32]{3,2,1,0:T(2,128)(2,1)S(1)}, u32[]{:S(2)}, u32[]{:S(2)}) async-start(bf16[16,2,2,32]{3,2,1,0:T(2,128)(2,1)} %bitcast.25), calls=%async_computation.2 | async-start | bytes 32768 | tf_op jit(solution)/shard_map/all_to_all | solution.py:86
  68.1 16.6 %all-to-all-start = ((bf16[16,2,2,512]{3,2,1,0:T(2,128)(2,1)}), bf16[16,2,2,512]{3,2,1,0:T(2,128)(2,1)S(1)}, u32[]{:S(2)}, u32[]{:S(2)}) async-start(bf16[16,2,2,512]{3,2,1,0:T(2,128)(2,1)} %bitcast.5), calls=%async_computation | async-start | bytes 131072 | tf_op jit(solution)/shard_map/all_to_all | solution.py:85
  84.6 8.7 %copy-start.6 = (s32[16]{0:T(128)S(1)}, s32[16]{0:T(128)}, u32[]{:S(2)}) copy-start(s32[16]{0:T(128)} %param.11) | copy-start | bytes 196
  84.7 10.1 %copy-start.4 = (bf16[256,1024]{1,0:T(8,128)(2,1)S(1)}, bf16[256,1024]{1,0:T(8,128)(2,1)}, u32[]{:S(2)}) copy-start(bf16[256,1024]{1,0:T(8,128)(2,1)} %param.16) | copy-start | bytes 1572868
  84.7 302.9 %all-to-all-start.1 = ((bf16[16,1,1024,512]{3,2,1,0:T(8,128)(2,1)}), bf16[16,1,1024,512]{3,2,1,0:T(8,128)(2,1)}, u32[]{:S(2)}, u32[]{:S(2)}) async-start(bf16[16,1,1024,512]{3,2,1,0:T(8,128)(2,1)} %bitcast.108), calls=%async_computation.1 | async-start | bytes 33554432 | tf_op jit(solution)/shard_map/all_to_all | solution.py:91
  429.5 87.8 %copy-start.7 = (u32[32]{0:T(128)S(1)}, u32[32]{0:T(128)}, u32[]{:S(2)}) copy-start(u32[32]{0:T(128)} %constant.73) | copy-start | bytes 388
  447.1 77.1 %all-to-all-start.3 = ((bf16[16,2,1024]{2,1,0:T(2,128)(2,1)}), bf16[16,2,1024]{2,1,0:T(2,128)(2,1)S(1)}, u32[]{:S(2)}, u32[]{:S(2)}) async-start(bf16[16,2,1024]{2,1,0:T(2,128)(2,1)} %reshape.242), calls=%async_computation.3 | async-start | bytes 131072 | tf_op jit(solution)/shard_map/all_to_all | solution.py:97
  534.2 85.3 %copy-start.1 = (bf16[256,1024]{1,0:T(8,128)(2,1)S(1)}, bf16[256,1024]{1,0:T(8,128)(2,1)}, u32[]{:S(2)}) copy-start(bf16[256,1024]{1,0:T(8,128)(2,1)} %param.15) | copy-start | bytes 1572868
Sparse Core Ops, SparseCore 0:
  9.5 40.6 all-gather.1
where the time goes:
time: 627 us; the launch traced here: 626 us
  waiting for transfers between devices  343 us (55%)
  starting transfers between devices  83.5 us (13%)
  blocking collectives  72.4 us (12%)
  local copies, waits for them, and re-layouts  52.9 us (8%)
  matrix products  48.3 us (8%)
  between operations  16.3 us (3%)
  other arithmetic  9.58 us (2%)
    all_to_all x1, waiting for transfers between devices, local(): lax.all_to_all(outgoing, 'xfer', split_axis=0, concat_axis=2, tiled=True)  290 us
    unnamed x1, blocking collectives  72.4 us
    all_to_all x1, starting transfers between devices, local(): lax.all_to_all(head_out, 'xfer', split_axis=2, concat_axis=0, tiled=True)  70.2 us
    all_gather x1, waiting for transfers between devices, local(): piece = lax.all_gather(hidden_in, 'xfer', axis=0, tiled=True)  42.1 us
    dot_general x1, matrix products, decode_attention(): jnp.einsum('isthr,ilr->isthl', absorbed, cache[..., :rank].astype(jnp.flo...  23.7 us
    unnamed x19, local copies, waits for them, and re-layouts  18.5 us
    gather x1, local copies, waits for them, and re-layouts, local(): outgoing = latent_cache[target_requests][:, None]  13 us
  transfers between devices with their start and end apart: 5, of which 4 were waited for; matrix products, arithmetic and copies ran while one was open for 3% of the time, Pallas kernels for 0%

commit v1 on v0

v1 whole, which is shorter than its diff:
```python
import functools

import jax
import jax.numpy as jnp
from jax import lax
from jax.experimental import pallas as pl
from jax.experimental.pallas import tpu as pltpu
from jax.sharding import PartitionSpec as P

HEADS = 64
KVH = 8
HD = 128
R = 16
NEG = -1e30
BF = jnp.bfloat16
F32 = jnp.float32


def dot_nt(a, b):
    return lax.dot_general(a, b, (((1,), (1,)), ((), ())), preferred_element_type=F32)


def flash_kernel(hl, lengths_ref, where_ref, q_ref, fresh_ref, cache_ref, upk_ref, upv_ref,
                 o_ref, lse_ref, hi_ref, lo_ref, lat_ref):
    ndevs, _, per, _ = q_ref.shape
    rank = upk_ref.shape[1]
    rows = ndevs * per
    each = ndevs // KVH
    positions = cache_ref.shape[1]
    req = pl.program_id(0)

    @pl.when(req == 0)
    def _():
        for g in range(KVH):
            qg = q_ref[g * each:(g + 1) * each].reshape(each * R * per, HD)
            a = jnp.dot(qg, upk_ref[g * HD:(g + 1) * HD], preferred_element_type=F32)
            a = a * (HD ** -0.5)
            hi = a.astype(BF)
            lo = (a - hi.astype(F32)).astype(BF)
            hi_ref[g * each:(g + 1) * each] = hi.reshape(each, R, per, rank)
            lo_ref[g * each:(g + 1) * each] = lo.reshape(each, R, per, rank)

    first = where_ref[0] * positions
    seen = lengths_ref[req] - first
    last = where_ref[0] == where_ref[1] - 1

    qh = hi_ref[:, pl.ds(req, 1)].reshape(rows, rank)
    ql = lo_ref[:, pl.ds(req, 1)].reshape(rows, rank)
    key = cache_ref[0, :, :rank]
    val = cache_ref[0, :, rank:]
    s = dot_nt(qh, key) + dot_nt(ql, key)
    pos = lax.broadcasted_iota(jnp.int32, s.shape, 1)
    s = jnp.where(pos < seen, s, NEG)
    fk = fresh_ref[0, :, :rank]
    fv = fresh_ref[0, :, rank:]
    n = dot_nt(qh, fk) + dot_nt(ql, fk)
    row = lax.broadcasted_iota(jnp.int32, n.shape, 0) % per
    col = lax.broadcasted_iota(jnp.int32, n.shape, 1)
    rs, rt = row // (2 * hl), (row // hl) % 2
    ok = (rs == col // 2) & (col % 2 <= rt) & last
    n = jnp.where(ok, n, NEG)
    top = jnp.maximum(jnp.max(s, axis=1, keepdims=True), jnp.max(n, axis=1, keepdims=True))
    p = jnp.exp(s - top)
    pn = jnp.exp(n - top)
    total = jnp.sum(p, axis=1, keepdims=True) + jnp.sum(pn, axis=1, keepdims=True)
    acc = jnp.dot(p.astype(BF), val, preferred_element_type=F32)
    acc = acc + jnp.dot(pn.astype(BF), fv, preferred_element_type=F32)
    lat_ref[:, pl.ds(req, 1)] = (acc / total).astype(BF).reshape(ndevs, 1, per, rank)
    lse_ref[0] = jnp.broadcast_to(top + jnp.log(total), (rows, 128))

    @pl.when(req == R - 1)
    def _():
        for g in range(KVH):
            lg = lat_ref[g * each:(g + 1) * each].reshape(each * R * per, rank)
            o = jnp.dot(lg, upv_ref[:, g * HD:(g + 1) * HD], preferred_element_type=F32)
            o_ref[g * each:(g + 1) * each] = o.astype(BF).reshape(each, R, per, HD)


def flash(q, fresh, cache, lengths, upk, upv, mine, ndevs, hl):
    _, _, per, _ = q.shape
    rank = upv.shape[0]
    rows = ndevs * per
    positions = cache.shape[1]
    where = jnp.stack([mine, jnp.full_like(mine, ndevs)]).astype(jnp.int32)
    whole = lambda a: pl.BlockSpec(a.shape, lambda i, *_: (0,) * a.ndim)
    return pl.pallas_call(
        functools.partial(flash_kernel, hl),
        out_shape=(
            jax.ShapeDtypeStruct((ndevs, R, per, HD), BF),
            jax.ShapeDtypeStruct((R, rows, 128), F32),
        ),
        grid_spec=pltpu.PrefetchScalarGridSpec(
            num_scalar_prefetch=2,
            grid=(R,),
            in_specs=[
                whole(q),
                pl.BlockSpec((1,) + fresh.shape[1:], lambda i, *_: (i, 0, 0)),
                pl.BlockSpec((1, positions, 2 * rank), lambda i, *_: (i, 0, 0)),
                whole(upk),
                whole(upv),
            ],
            out_specs=[
                pl.BlockSpec((ndevs, R, per, HD), lambda i, *_: (0, 0, 0, 0)),
                pl.BlockSpec((1, rows, 128), lambda i, *_: (i, 0, 0)),
            ],
            scratch_shapes=[
                pltpu.VMEM((ndevs, R, per, rank), BF),
                pltpu.VMEM((ndevs, R, per, rank), BF),
                pltpu.VMEM((ndevs, R, per, rank), BF),
            ],
        ),
        compiler_params=pltpu.CompilerParams(vmem_limit_bytes=56 * 2 ** 20),
        cost_estimate=pl.CostEstimate(
            flops=2 * R * rows * positions * rank * 3,
            bytes_accessed=cache.size * 2,
            transcendentals=R * rows * positions,
        ),
        name="flash",
    )(lengths, where, q, fresh, cache, upk, upv)


def local(hidden_in, latent_cache, lengths, placement, w_query, w_down, up_key, up_value, w_out):
    ndevs = lax.axis_size("xfer")
    mine = lax.axis_index("xfer")
    rank = up_key.shape[0]
    width = hidden_in.shape[2]
    hl = w_query.shape[1] // HD
    slot_rows = hidden_in.shape[0]
    samples = slot_rows * ndevs // R
    nrows = slot_rows * 2 * ndevs
    per = samples * 2 * hl
    x = lax.all_gather(hidden_in.reshape(slot_rows * 2, width), "xfer", axis=0, tiled=True)
    query = jnp.dot(x, w_query, preferred_element_type=F32).astype(BF)
    fresh = jnp.dot(x, w_down, preferred_element_type=F32).astype(BF)
    q = lax.all_gather(query.reshape(R, per, HD), "xfer", axis=0)
    own = lax.all_gather(fresh, "xfer", axis=1, tiled=True)
    own = own.reshape(R, samples * 2, 2 * rank)
    pad = -(samples * 2) % 16
    own = jnp.pad(own, ((0, 0), (0, pad), (0, 0)))
    o, lse = flash(q, own, latent_cache, lengths, up_key.T, up_value, mine, ndevs, hl)
    lse = lse[:, :, 0].reshape(R, ndevs, per).transpose(1, 0, 2)
    o = lax.all_to_all(o, "xfer", split_axis=0, concat_axis=0, tiled=True)
    lse = lax.all_to_all(lse, "xfer", split_axis=0, concat_axis=0, tiled=True)
    share = jax.nn.softmax(lse, axis=0)
    head_out = jnp.sum(o.astype(F32) * share[..., None], axis=0).astype(BF)
    head_out = head_out.reshape(R, samples * 2, hl * HD)[placement].reshape(nrows, hl * HD)
    part = jnp.dot(head_out, w_out, preferred_element_type=F32).astype(BF)
    part = lax.all_to_all(
        part.reshape(ndevs, slot_rows * 2, width), "xfer", split_axis=0, concat_axis=0, tiled=True
    )
    summed = jnp.sum(part.astype(F32), axis=0).astype(BF)
    return summed.reshape(slot_rows, 2, width)


def solution(mesh):
    placed = (
        P(("parts", "xfer"), None, None),
        P("parts", "xfer", None),
        P("parts"),
        P("parts"),
        P(None, "xfer"),
        P(None, "xfer"),
        P(),
        P(),
        P("xfer", None),
    )
    return jax.shard_map(
        local,
        mesh=mesh,
        in_specs=placed,
        out_specs=P(("parts", "xfer"), None, None),
        check_vma=False,
    )
```

time: 627 us -> 207 us (0.33)
  waiting for transfers between devices: 343 us -> 77.9 us
  starting transfers between devices: 83.5 us -> 3.7 us
  local copies, waits for them, and re-layouts: 52.9 us -> 10.3 us
  matrix products: 48.3 us -> 10.3 us
  Pallas kernels: 0 us -> 26.6 us
  blocking collectives: 72.4 us -> 61.2 us
  other arithmetic: 9.58 us -> 2.55 us
    all_to_all x4 -> x1, waiting for transfers between devices: 301 us -> 21.5 us  [local(): o = lax.all_to_all(o, 'xfer', split_axis=0, concat_axis=0, tiled=True)]
    all_to_all x4 -> x1, starting transfers between devices: 83.5 us -> 3.65 us  [local(): o = lax.all_to_all(o, 'xfer', split_axis=0, concat_axis=0, tiled=True)]
    unnamed x1 -> x0, blocking collectives: 72.4 us -> none
    all_to_all x0 -> x2, blocking collectives: none -> 41.4 us  [the longest x1 31.5 us: local(): lax.all_to_all(part.reshape(ndevs, slot_rows * 2, width), 'xfer', split_a...]
    dot_general x9 -> x3, matrix products: 48.3 us -> 10.3 us  [the longest x1 4.99 us: local(): query = jnp.dot(x, w_query, preferred_element_type=F32).astype(BF)]
    pallas_call x0 -> x1, Pallas kernels: none -> 26.6 us  [flash(): pl.pallas_call(functools.partial(flash_kernel, hl), out_shape=(jax.ShapeD...]
    all_gather x0 -> x1, blocking collectives: none -> 19.9 us  [local(): own = lax.all_gather(fresh, 'xfer', axis=1, tiled=True)]
    gather x4 -> x1, local copies, waits for them, and re-layouts: 15 us -> 0.61 us  [local(): head_out.reshape(R, samples * 2, hl * HD)[placement].reshape(nrows, hl * HD)]
  transfers between devices with their start and end apart: 5 -> 3, of which waited for: 4 -> 3; matrix products, arithmetic and copies ran while one was open for 3% -> 2% of each run, Pallas kernels for 0% -> 0%
where the time goes in v1:
time: 207 us; the launch traced here: 206 us
  waiting for transfers between devices  77.9 us (38%)
  blocking collectives  61.2 us (30%)
  Pallas kernels  26.6 us (13%)
  between operations  13.6 us (7%)
  local copies, waits for them, and re-layouts  10.3 us (5%)
  matrix products  10.3 us (5%)
  starting transfers between devices  3.7 us (2%)
  other arithmetic  2.55 us (1%)
    all_gather x1, waiting for transfers between devices, local(): lax.all_gather(hidden_in.reshape(slot_rows * 2, width), 'xfer', axis=0, t...  42 us
    all_to_all x1, blocking collectives, local(): lax.all_to_all(part.reshape(ndevs, slot_rows * 2, width), 'xfer', split_a...  31.5 us
    pallas_call x1, Pallas kernels, flash(): pl.pallas_call(functools.partial(flash_kernel, hl), out_shape=(jax.ShapeD...  26.6 us
    all_to_all x1, waiting for transfers between devices, local(): o = lax.all_to_all(o, 'xfer', split_axis=0, concat_axis=0, tiled=True)  21.5 us
    all_gather x1, blocking collectives, local(): own = lax.all_gather(fresh, 'xfer', axis=1, tiled=True)  19.9 us
    all_gather x1, waiting for transfers between devices, local(): q = lax.all_gather(query.reshape(R, per, HD), 'xfer', axis=0)  14.4 us
    all_to_all x1, blocking collectives, local(): lse = lax.all_to_all(lse, 'xfer', split_axis=0, concat_axis=0, tiled=True)  9.92 us
    dot_general x1, matrix products, local(): query = jnp.dot(x, w_query, preferred_element_type=F32).astype(BF)  4.99 us
  transfers between devices with their start and end apart: 3, of which 3 were waited for; matrix products, arithmetic and copies ran while one was open for 2% of the time, Pallas kernels for 0%

profile of v1, /device:TPU:0, one launch (start us, length us, event | category | flops | bytes accessed | tf_op | source)
XLA Modules:
  0.0 206.2 jit_solution(7210630042935496322)
XLA Ops:
  6.5 0.0 copy-start
  6.5 0.0 all-gather.6.cloned.1.call-start
  6.5 1.6 reshape.35
  8.1 0.0 all-gather.6.cloned.1.call-update
  8.1 0.0 all-gather.4.cloned.1.call-start
  8.2 42.0 %all-gather.6.cloned.1.call-done = bf16[16,4,8192]{2,1,0:T(4,128)(2,1)} async-done(((bf16[1,4,8192]{2,1,0:T(4,128)(2,1)}), bf16[16,4,8192]{2,1,0:T(4,128)(2,1)}) %all-gather.6.cloned.1.call-update) | async-done | bytes 1048592 | tf_op jit(solution)/shard_map/all_gather | solution.py:132
  50.2 1.3 reshape.36
  51.5 0.0 copy-start.1
  51.5 5.0 %convolution_convert_fusion.1 = bf16[64,512]{1,0:T(8,128)(2,1)S(1)} fusion(bf16[64,8192]{1,0:T(8,128)(2,1)S(1)} %reshape.36, bf16[8192,512]{1,0:T(8,128)(2,1)} %param.13), kind=kOutput, calls=%fused_computation.4 | convolution fusion | flops 536903680 | bytes 9502720 | tf_op jit(solution)/shard_map/dot_general | solution.py:133
  56.5 0.7 all_gather_reshape.3
  57.2 0.0 all-gather.4.cloned.1.call-update
  57.3 0.0 copy-done.1
  57.3 1.0 copy.17
  58.3 0.6 pad_add_fusion.where_ref
  58.9 0.0 copy-done
  58.9 0.4 convolution_convert_fusion.2
  59.3 19.9 %all_gather.11 = bf16[64,512]{0,1:T(8,128)(2,1)S(1)} all-gather(bf16[64,32]{0,1:T(8,128)(2,1)S(1)} %convolution_convert_fusion.2), channel_id=1, replica_groups=mesh['parts'=2,'xfer'=16] {'xfer'}, dimensions={1}, use_global_device_ids=true | all-gather | bytes 69632 | tf_op jit(solution)/shard_map/all_gather | solution.py:136
  79.1 0.1 copy.16
  79.2 0.7 pad.4.fresh_ref
  80.0 14.4 %all-gather.4.cloned.1.call-done.q_ref = bf16[16,16,16,128]{3,2,1,0:T(8,128)(2,1)} async-done(((bf16[1,16,16,128]{3,2,1,0:T(8,128)(2,1)}), bf16[16,16,16,128]{3,2,1,0:T(8,128)(2,1)}) %all-gather.4.cloned.1.call-update) | async-done | bytes 1048592 | tf_op jit(solution)/shard_map/all_gather | solution.py:135
  94.4 0.0 copy-start.2
  94.4 26.6 %flash.1 = (bf16[16,16,16,128]{3,2,1,0:T(8,128)(2,1)}, f32[16,256,128]{2,1,0:T(8,128)}) custom-call(s32[16]{0:T(128)} %lengths_ref.1, s32[2]{0:T(128)} %pad_add_fusion.where_ref, bf16[16,16,16,128]{3,2,1,0:T(8,128)(2,1)} %all-gather.4.cloned.1.call-done.q_ref, bf16[16,16,512]{2,1,0:T(8,128)(2,1)} %pad.4.fresh_ref, bf16[16,1024,512]{2,1,0:T(8,128)(2,1)} %cache_ref.1, ...), custom_call_target="tpu_custom_call" | custom-call | flops 6442450944 | bytes 16777216 | tf_op jit(solution)/shard_map/flash/pallas_call | solution.py:86
  121.0 2.2 %slice_reduce_fusion = f32[16,256]{1,0:T(8,128)S(1)} fusion(f32[16,256,128]{2,1,0:T(8,128)} %get-tuple-element.8), kind=kLoop, calls=%fused_computation.3 | loop fusion | bytes 32768 | tf_op jit(solution)/shard_map/slice | solution.py:141
  123.2 0.1 reshape_squeeze.3
  123.4 0.1 reshape.39
  123.5 9.9 %all_to_all.15 = f32[16,1,256]{2,1,0:T(1,128)S(1)} all-to-all(f32[16,1,256]{2,1,0:T(1,128)S(1)} %reshape.39), channel_id=1, replica_groups=mesh['parts'=2,'xfer'=16] {'xfer'}, dimensions={0} | all-to-all | bytes 32768 | tf_op jit(solution)/shard_map/all_to_all | solution.py:143
  133.4 3.7 %all-to-all-start = ((bf16[16,16,16,128]{3,2,1,0:T(8,128)(2,1)}), bf16[16,16,16,128]{3,2,1,0:T(8,128)(2,1)S(1)}, u32[]{:S(2)}, u32[]{:S(2)}) async-start(bf16[16,16,16,128]{3,2,1,0:T(8,128)(2,1)} %get-tuple-element.7), calls=%async_computation | async-start | bytes 2097152 | tf_op jit(solution)/shard_map/all_to_all | solution.py:142
  137.1 0.0 copy-done.2
  137.1 0.5 broadcast.20
  137.6 0.7 reduce.3
  138.3 0.1 reshape.40
  138.5 21.5 %all-to-all-done = bf16[16,16,16,128]{3,2,1,0:T(8,128)(2,1)S(1)} async-done(((bf16[16,16,16,128]{3,2,1,0:T(8,128)(2,1)}), bf16[16,16,16,128]{3,2,1,0:T(8,128)(2,1)S(1)}, u32[]{:S(2)}, u32[]{:S(2)}) %all-to-all-start) | async-done | bytes 1048608 | tf_op jit(solution)/shard_map/all_to_all | solution.py:142
  159.9 0.7 multiply_reduce_fusion
  160.7 0.6 gather_fusion
  161.3 5.0 %convolution_convert_fusion = bf16[64,8192]{1,0:T(8,128)(2,1)S(1)} fusion(bf16[64,512]{1,0:T(8,128)(2,1)S(1)} %reshape.23, bf16[512,8192]{1,0:T(8,128)(2,1)} %param.17), kind=kOutput, calls=%fused_computation.1 | convolution fusion | flops 537395200 | bytes 9502720 | tf_op jit(solution)/shard_map/dot_general | solution.py:147
  166.3 0.4 reshape.24
  166.7 31.5 %all_to_all.16 = bf16[16,4,8192]{2,1,0:T(4,128)(2,1)S(1)} all-to-all(bf16[16,4,8192]{2,1,0:T(4,128)(2,1)S(1)} %reshape.24), channel_id=1, replica_groups=mesh['parts'=2,'xfer'=16] {'xfer'}, dimensions={0} | all-to-all | bytes 2097152 | tf_op jit(solution)/shard_map/all_to_all | solution.py:148
  198.2 0.5 reduce_sum.32
  198.7 0.7 reshape.25
  (9 shorter events, 0.2 us)
Async XLA Ops:
  6.5 52.3 %copy-start = (bf16[8192,32]{0,1:T(8,128)(2,1)S(1)}, bf16[8192,32]{0,1:T(8,128)(2,1)}, u32[]{:S(2)}) copy-start(bf16[8192,32]{0,1:T(8,128)(2,1)} %param.14) | copy-start | bytes 1572868
  6.5 43.7 %all-gather.6.cloned.1.call-start = ((), (), s32[]{:S(2)}) async-start(), calls=%async_computation.4 | async-start | bytes 1114112 | tf_op jit(solution)/shard_map/all_gather | solution.py:132
  8.1 86.2 %all-gather.4.cloned.1.call-start = ((), (), s32[]{:S(2)}) async-start(), calls=%async_computation.3 | async-start | bytes 1114112 | tf_op jit(solution)/shard_map/all_gather | solution.py:135
  51.5 5.7 %copy-start.1 = (bf16[256,1024]{1,0:T(8,128)(2,1)S(1)}, bf16[256,1024]{1,0:T(8,128)(2,1)}, u32[]{:S(2)}) copy-start(bf16[256,1024]{1,0:T(8,128)(2,1)} %param.15) | copy-start | bytes 1572868
  94.4 42.7 %copy-start.2 = (s32[16]{0:T(128)S(1)}, s32[16]{0:T(128)}, u32[]{:S(2)}) copy-start(s32[16]{0:T(128)} %param.12) | copy-start | bytes 196
  133.4 26.6 %all-to-all-start = ((bf16[16,16,16,128]{3,2,1,0:T(8,128)(2,1)}), bf16[16,16,16,128]{3,2,1,0:T(8,128)(2,1)S(1)}, u32[]{:S(2)}, u32[]{:S(2)}) async-start(bf16[16,16,16,128]{3,2,1,0:T(8,128)(2,1)} %get-tuple-element.7), calls=%async_computation | async-start | bytes 2097152 | tf_op jit(solution)/shard_map/all_to_all | solution.py:142
Sparse Core Ops, SparseCore 0:
  9.5 40.6 all-gather.5
  57.4 36.9 all-gather.3

commit v2 on v1

--- a/solution.py
+++ b/solution.py
@@ -119,37 +119,329 @@
     )(lengths, where, q, fresh, cache, upk, upv)
 
 
+def place(ndevs):
+    me = lax.axis_index("xfer")
+    return me // 4, (me // 2) % 2, me % 2
+
+
+def index_of(z, y, c):
+    return z * 4 + y * 2 + c
+
+
+def greet(ndevs):
+    deep = ndevs // 4
+    z, y, c = place(ndevs)
+    barrier = pltpu.get_barrier_semaphore()
+    peers = [index_of((z + k) % deep, y, c) for k in range(1, deep)]
+    peers += [index_of(z, 1 - y, c), index_of(z, y, 1 - c)]
+    for peer in peers:
+        pl.semaphore_signal(barrier, inc=1, device_id={"xfer": peer}, device_id_type=pl.DeviceIdType.MESH)
+    pl.semaphore_wait(barrier, len(peers))
+
+
+def remote(src, dst, send, recv, peer):
+    return pltpu.make_async_remote_copy(
+        src_ref=src, dst_ref=dst, send_sem=send, recv_sem=recv,
+        device_id={"xfer": peer}, device_id_type=pl.DeviceIdType.MESH,
+    )
+
+
+def spread(ndevs, buf, send, recv):
+    deep = ndevs // 4
+    z, y, c = place(ndevs)
+    far, near, twin = 0, deep, 2 * deep
+
+    def move(block, slot, peer):
+        return remote(buf.at[block], buf.at[block], send.at[slot], recv.at[slot], peer)
+
+    mine = index_of(z, y, c)
+    along = [move(mine, far + k, index_of((z + k) % deep, y, c)) for k in range(1, deep)]
+    for copy in along:
+        copy.start()
+    across, over = [], []
+    for k in range(deep + 1):
+        if k < deep:
+            block = index_of((z - k + deep) % deep, y, c)
+            if k:
+                along[k - 1].wait_recv()
+            across.append(move(block, near + k, index_of(z, 1 - y, c)))
+            across[-1].start()
+            over.append(move(block, twin + k, index_of(z, y, 1 - c)))
+            over[-1].start()
+        if k:
+            across[k - 1].wait_recv()
+            block = index_of((z - k + 1 + deep) % deep, 1 - y, c)
+            over.append(move(block, twin + deep + k - 1, index_of(z, y, 1 - c)))
+            over[-1].start()
+    for copy in over:
+        copy.wait_recv()
+    for copy in along + across + over:
+        copy.wait_send()
+
+
+def project_kernel(ndevs, hidden_ref, wq_ref, wd_ref, out_ref,
+                   x_ref, wide_ref, wqv_ref, wdv_ref, stage_ref, send, recv, send2, recv2, wsem):
+    copies = [
+        pltpu.make_async_copy(wq_ref, wqv_ref, wsem.at[0]),
+        pltpu.make_async_copy(wd_ref, wdv_ref, wsem.at[1]),
+    ]
+    for copy in copies:
+        copy.start()
+    me = lax.axis_index("xfer")
+    slots, _, width = hidden_ref.shape
+    tiles = width // HD
+    nrows = ndevs * slots * 2
+    hl = wqv_ref.shape[1] // HD
+    fw = wdv_ref.shape[1]
+    for s in range(slots):
+        for t in range(tiles):
+            wide_ref[pl.ds(s * 2 * tiles + t, 2, stride=tiles), :] = (
+                hidden_ref[s, :, t * HD:(t + 1) * HD].astype(F32))
+    x_ref[pl.ds(me, 1)] = wide_ref[:slots * 2 * tiles, :].astype(BF)[None]
+    greet(ndevs)
+    spread(ndevs, x_ref, send, recv)
+    wide_ref[...] = x_ref[...].astype(F32).reshape(wide_ref.shape)
+    for copy in copies:
+        copy.wait()
+    query = jnp.zeros((nrows, hl * HD), F32)
+    fresh = jnp.zeros((nrows, fw), F32)
+    step = 16
+    for t in range(0, tiles, step):
+        xt = jnp.concatenate(
+            [wide_ref[pl.ds(t + i, nrows, stride=tiles), :].astype(BF) for i in range(step)], axis=1)
+        span = slice(t * HD, (t + step) * HD)
+        query = query + jnp.dot(xt, wqv_ref[span], preferred_element_type=F32)
+        fresh = fresh + jnp.dot(xt, wdv_ref[span], preferred_element_type=F32)
+    for h in range(hl):
+        stage_ref[pl.ds(h, nrows, stride=hl), :] = query[:, h * HD:(h + 1) * HD]
+    stage_ref[nrows * hl:, :] = jnp.zeros((nrows, HD), F32)
+    stage_ref[nrows * hl:, :fw] = fresh
+    out_ref[pl.ds(me, 1)] = stage_ref[...].astype(BF)[None]
+    spread(ndevs, out_ref, send2, recv2)
+
+
+def project(hidden, wq, wd, ndevs):
+    slots, _, width = hidden.shape
+    tall = slots * 2 * width // HD
+    nrows = ndevs * slots * 2
+    hl = wq.shape[1] // HD
+    sems = pltpu.SemaphoreType.DMA((ndevs,))
+    return pl.pallas_call(
+        functools.partial(project_kernel, ndevs),
+        out_shape=jax.ShapeDtypeStruct((ndevs, nrows * (hl + 1), HD), BF),
+        in_specs=[
+            pl.BlockSpec(memory_space=pltpu.VMEM),
+            pl.BlockSpec(memory_space=pl.ANY),
+            pl.BlockSpec(memory_space=pl.ANY),
+        ],
+        out_specs=pl.BlockSpec(memory_space=pltpu.VMEM),
+        scratch_shapes=[
+            pltpu.VMEM((ndevs, tall, HD), BF),
+            pltpu.VMEM((ndevs * tall, HD), F32),
+            pltpu.VMEM(wq.shape, BF),
+            pltpu.VMEM(wd.shape, BF),
+            pltpu.VMEM((nrows * (hl + 1), HD), F32),
+            sems, sems, sems, sems,
+            pltpu.SemaphoreType.DMA((2,)),
+        ],
+        compiler_params=pltpu.CompilerParams(
+            collective_id=0, has_side_effects=True, vmem_limit_bytes=56 * 2 ** 20),
+        name="project",
+    )(hidden, wq, wd)
+
+
+def fold(ndevs, blocks, held1, held2, held3, send, recv, merge, finish):
+    deep = ndevs // 4
+    z, y, c = place(ndevs)
+    many = len(blocks)
+    at = lambda refs, i: [r.at[i] for r in refs]
+    count = [0]
+
+    def ship(src, dst, peer):
+        copies = []
+        for s, d in zip(src, dst):
+            copies.append(remote(s, d, send.at[count[0]], recv.at[count[0]], peer))
+            count[0] += 1
+        for copy in copies:
+            copy.start()
+        return copies
+
+    def arrive(copies):
+        for copy in copies:
+            copy.wait_recv()
+
+    order = [(z + k) % deep for k in range(1, deep + 1)]
+    twin = index_of(z, y, 1 - c)
+    first = []
+    for far in (1, 0):
+        yy = 1 - y if far else y
+        for k in range(deep):
+            first.append(ship(at(blocks, index_of(order[k], yy, 1 - c)), at(held1, far * deep + k), twin))
+    second = []
+    for k in range(deep):
+        arrive(first[k])
+        here = at(blocks, index_of(order[k], 1 - y, c))
+        merge(here, here, at(held1, deep + k))
+        second.append(ship(here, at(held2, k), index_of(z, 1 - y, c)))
+    for k in range(deep):
+        arrive(first[deep + k])
+        here = at(blocks, index_of(order[k], y, c))
+        merge(here, here, at(held1, k))
+    third = []
+    for k in range(deep):
+        arrive(second[k])
+        here = at(blocks, index_of(order[k], y, c))
+        merge(here, here, at(held2, k))
+        if k < deep - 1:
+            third.append(ship(here, at(held3, k), index_of(order[k], y, c)))
+    for copies in third:
+        arrive(copies)
+    finish(at(blocks, index_of(z, y, c)), [at(held3, k) for k in range(deep - 1)])
+    for copies in first + second + third:
+        for copy in copies:
+            copy.wait_send()
+
+
+def turn(w):
+    return jnp.transpose(jnp.broadcast_to(w, (HD, HD)))
+
+
+def merge_heads(dst, a, b):
+    n = a[0].shape[0] // HD
+    la, lb = a[1][...], b[1][...]
+    top = jnp.maximum(la, lb)
+    ea, eb = jnp.exp(la - top), jnp.exp(lb - top)
+    both = ea + eb
+    share = ea / both
+    lse = top + jnp.log(both)
+    for t in range(n):
+        span = slice(t * HD, (t + 1) * HD)
+        oa, ob = a[0][span].astype(F32), b[0][span].astype(F32)
+        dst[0][span] = (ob + turn(share[t:t + 1]) * (oa - ob)).astype(BF)
+    dst[1][...] = lse
+
+
+def merge_sums(dst, a, b):
+    dst[0][...] = (a[0][...].astype(F32) + b[0][...].astype(F32)).astype(BF)
+
+
+def finish_kernel(ndevs, o_ref, l_ref, perm_ref, wo_ref, out_ref,
+                  ob_ref, lb_ref, o1, l1, o2, l2, o3, l3, wov_ref, head_ref, wide_ref, *rest):
+    pieces = (len(rest) - 3) // 4
+    sums = rest[:4 * pieces]
+    send, recv, wsem = rest[-3:]
+    copies = [
+        pltpu.make_async_copy(wo_ref, wov_ref, wsem.at[0]),
+    ]
+    for copy in copies:
+        copy.start()
+    deep = ndevs // 4
+    slots, _, width = out_ref.shape
+    nrows = ndevs * slots * 2
+    hl = wov_ref.shape[0] // HD
+    tiles = width // HD // pieces
+    ob_ref[...] = o_ref[...]
+    lb_ref[...] = l_ref[...]
+    greet(ndevs)
+
+    def finish_heads(mine, others):
+        n = mine[0].shape[0] // HD
+        ls = [mine[1][...]] + [o[1][...] for o in others]
+        top = functools.reduce(jnp.maximum, ls)
+        es = [jnp.exp(l - top) for l in ls]
+        both = functools.reduce(jnp.add, es)
+        for t in range(n):
+            span = slice(t * HD, (t + 1) * HD)
+            got = jnp.zeros((HD, HD), F32)
+            for e, o in zip(es, [mine] + list(others)):
+                got = got + turn((e / both)[t:t + 1]) * o[0][span].astype(F32)
+            head_ref[span] = got
+
+    fold(ndevs, (ob_ref, lb_ref), (o1, l1), (o2, l2), (o3, l3),
+         send.at[0], recv.at[0], merge_heads, finish_heads)
+    heads = [head_ref[pl.ds(h, nrows, stride=hl), :].astype(BF) for h in range(hl)]
+    head = jnp.concatenate(heads, axis=1)
+    head = jnp.dot(perm_ref[...], head, preferred_element_type=F32).astype(BF)
+    for copy in copies:
+        copy.wait()
+    for p in range(pieces):
+        step = 8
+        for t in range(0, tiles, step):
+            at = (p * tiles + t) * HD
+            got = jnp.dot(head, wov_ref[:, at:at + step * HD], preferred_element_type=F32)
+            for i in range(step):
+                wide_ref[pl.ds(t + i, nrows, stride=tiles), :] = got[:, i * HD:(i + 1) * HD]
+        buf = sums[4 * p]
+        buf[...] = wide_ref[...].astype(BF).reshape(buf.shape)
+
+        def finish_sums(mine, others, p=p):
+            total = mine[0][...].astype(F32)
+            for o in others:
+                total = total + o[0][...].astype(F32)
+            wide_ref[:slots * 2 * tiles, :] = total
+            for s in range(slots):
+                for t in range(tiles):
+                    at = (p * tiles + t) * HD
+                    out_ref[s, :, at:at + HD] = (
+                        wide_ref[pl.ds(s * 2 * tiles + t, 2, stride=tiles), :].astype(BF))
+
+        fold(ndevs, (buf,), (sums[4 * p + 1],), (sums[4 * p + 2],), (sums[4 * p + 3],),
+             send.at[1 + p], recv.at[1 + p], merge_sums, finish_sums)
+
+
+def finish(o, lse, perm, wo, ndevs, slots, pieces=1):
+    width = wo.shape[1]
+    deep = ndevs // 4
+    rows = o.shape[1]
+    nrows = ndevs * slots * 2
+    tall = slots * 2 * width // HD // pieces
+    sizes = (ndevs, 2 * deep, deep, deep - 1)
+    scratch = [pltpu.VMEM(o.shape, BF), pltpu.VMEM(lse.shape, F32)]
+    for n in sizes[1:]:
+        scratch += [pltpu.VMEM((n, rows, HD), BF), pltpu.VMEM((n,) + lse.shape[1:], F32)]
+    scratch += [
+        pltpu.VMEM(wo.shape, BF),
+        pltpu.VMEM((rows, HD), F32),
+        pltpu.VMEM((ndevs * tall, HD), F32),
+    ]
+    for _ in range(pieces):
+        scratch += [pltpu.VMEM((n, tall, HD), BF) for n in sizes]
+    sems = pltpu.SemaphoreType.DMA((1 + pieces, 8 * deep))
+    scratch += [sems, sems, pltpu.SemaphoreType.DMA((1,))]
+    return pl.pallas_call(
+        functools.partial(finish_kernel, ndevs),
+        out_shape=jax.ShapeDtypeStruct((slots, 2, width), BF),
+        in_specs=[pl.BlockSpec(memory_space=pltpu.VMEM)] * 3 + [pl.BlockSpec(memory_space=pl.ANY)],
+        out_specs=pl.BlockSpec(memory_space=pltpu.VMEM),
+        scratch_shapes=scratch,
+        compiler_params=pltpu.CompilerParams(
+            collective_id=1, has_side_effects=True, vmem_limit_bytes=56 * 2 ** 20),
+        name="finish",
+    )(o, lse, perm, wo)
+
+
 def local(hidden_in, latent_cache, lengths, placement, w_query, w_down, up_key, up_value, w_out):
     ndevs = lax.axis_size("xfer")
     mine = lax.axis_index("xfer")
     rank = up_key.shape[0]
-    width = hidden_in.shape[2]
     hl = w_query.shape[1] // HD
+    fw = w_down.shape[1]
     slot_rows = hidden_in.shape[0]
     samples = slot_rows * ndevs // R
     nrows = slot_rows * 2 * ndevs
     per = samples * 2 * hl
-    x = lax.all_gather(hidden_in.reshape(slot_rows * 2, width), "xfer", axis=0, tiled=True)
-    query = jnp.dot(x, w_query, preferred_element_type=F32).astype(BF)
-    fresh = jnp.dot(x, w_down, preferred_element_type=F32).astype(BF)
-    q = lax.all_gather(query.reshape(R, per, HD), "xfer", axis=0)
-    own = lax.all_gather(fresh, "xfer", axis=1, tiled=True)
-    own = own.reshape(R, samples * 2, 2 * rank)
+    both = project(hidden_in, w_query, w_down, ndevs)
+    q = both[:, :nrows * hl].reshape(ndevs, R, per, HD)
+    own = both[:, nrows * hl:, :fw].transpose(1, 0, 2).reshape(R, samples * 2, 2 * rank)
     pad = -(samples * 2) % 16
     own = jnp.pad(own, ((0, 0), (0, pad), (0, 0)))
     o, lse = flash(q, own, latent_cache, lengths, up_key.T, up_value, mine, ndevs, hl)
-    lse = lse[:, :, 0].reshape(R, ndevs, per).transpose(1, 0, 2)
-    o = lax.all_to_all(o, "xfer", split_axis=0, concat_axis=0, tiled=True)
-    lse = lax.all_to_all(lse, "xfer", split_axis=0, concat_axis=0, tiled=True)
-    share = jax.nn.softmax(lse, axis=0)
-    head_out = jnp.sum(o.astype(F32) * share[..., None], axis=0).astype(BF)
-    head_out = head_out.reshape(R, samples * 2, hl * HD)[placement].reshape(nrows, hl * HD)
-    part = jnp.dot(head_out, w_out, preferred_element_type=F32).astype(BF)
-    part = lax.all_to_all(
-        part.reshape(ndevs, slot_rows * 2, width), "xfer", split_axis=0, concat_axis=0, tiled=True
-    )
-    summed = jnp.sum(part.astype(F32), axis=0).astype(BF)
-    return summed.reshape(slot_rows, 2, width)
+    lse = lse[:, :, 0].reshape(R, ndevs, per).transpose(1, 0, 2).reshape(ndevs, R * per // HD, HD)
+    lse = jnp.pad(lse, ((0, 0), (0, 8 - R * per // HD), (0, 0)))
+    slot = jnp.arange(nrows, dtype=jnp.int32)
+    source = jnp.repeat(placement, 2 * samples) * (2 * samples) + slot % (2 * samples)
+    perm = (source[:, None] == slot[None, :]).astype(BF)
+    return finish(o.reshape(ndevs, R * per, HD), lse, perm, w_out, ndevs, slot_rows)
 
 
 def solution(mesh):

time: 207 us -> 111 us (0.54)
  waiting for transfers between devices: 77.9 us -> 0 us
  Pallas kernels: 26.6 us -> 95.8 us
  blocking collectives: 61.2 us -> 0 us
  between operations: 13.6 us -> 0.08 us
  matrix products: 10.3 us -> 0 us
  starting transfers between devices: 3.7 us -> 0 us
  local copies, waits for them, and re-layouts: 10.3 us -> 13 us
    pallas_call x0 -> x2, Pallas kernels: none -> 69.3 us  [the longest x1 36.4 us: project(): pl.pallas_call(functools.partial(project_kernel, ndevs), out_shape=jax.Sh...]
    all_gather x2 -> x0, waiting for transfers between devices: 56.4 us -> none  [the longest x1 42 us: local(): lax.all_gather(hidden_in.reshape(slot_rows * 2, width), 'xfer', axis=0, t...]
    all_to_all x2 -> x0, blocking collectives: 41.4 us -> none  [the longest x1 31.5 us: local(): lax.all_to_all(part.reshape(ndevs, slot_rows * 2, width), 'xfer', split_a...]
    all_to_all x1 -> x0, waiting for transfers between devices: 21.5 us -> none  [local(): o = lax.all_to_all(o, 'xfer', split_axis=0, concat_axis=0, tiled=True)]
    all_gather x1 -> x0, blocking collectives: 19.9 us -> none  [local(): own = lax.all_gather(fresh, 'xfer', axis=1, tiled=True)]
    dot_general x3 -> x0, matrix products: 10.3 us -> none  [the longest x1 4.99 us: local(): query = jnp.dot(x, w_query, preferred_element_type=F32).astype(BF)]
    all_to_all x1 -> x0, starting transfers between devices: 3.65 us -> none  [local(): o = lax.all_to_all(o, 'xfer', split_axis=0, concat_axis=0, tiled=True)]
    slice x1 -> x2, local copies, waits for them, and re-layouts: 2.2 us -> 4.61 us  [the longest x1 2.4 us: local(): q = both[:, :nrows * hl].reshape(ndevs, R, per, HD)]
  transfers between devices with their start and end apart: 3 -> 0, of which waited for: 3 -> 0; matrix products, arithmetic and copies ran while one was open for 2% -> 0% of each run, Pallas kernels for 0% -> 0%
where the time goes in v2:
time: 111 us; the launch traced here: 110 us
  Pallas kernels  95.8 us (86%)
  local copies, waits for them, and re-layouts  13 us (12%)
  other arithmetic  1.33 us (1%)
    pallas_call x1, Pallas kernels, project(): pl.pallas_call(functools.partial(project_kernel, ndevs), out_shape=jax.Sh...  36.4 us
    pallas_call x1, Pallas kernels, finish(): pl.pallas_call(functools.partial(finish_kernel, ndevs), out_shape=jax.Sha...  32.9 us
    pallas_call x1, Pallas kernels, flash(): pl.pallas_call(functools.partial(flash_kernel, hl), out_shape=(jax.ShapeD...  26.5 us
    unnamed x7, local copies, waits for them, and re-layouts  5.22 us
    slice x1, local copies, waits for them, and re-layouts, local(): q = both[:, :nrows * hl].reshape(ndevs, R, per, HD)  2.4 us

profile of v2, /device:TPU:0, one launch (start us, length us, event | category | flops | bytes accessed | tf_op | source)
XLA Modules:
  0.0 110.2 jit_solution(5747963820106893009)
XLA Ops:
  0.0 2.7 %copy.14.wd_ref = bf16[8192,32]{1,0:T(8,128)(2,1)} copy(bf16[8192,32]{0,1:T(8,128)(2,1)} %param.14) | data formatting | bytes 1048576 | tf_op args[5]
  2.7 36.4 %project.1 = bf16[16,320,128]{2,1,0:T(8,128)(2,1)} custom-call(bf16[2,2,8192]{2,1,0:T(2,128)(2,1)} %hidden_ref.1, bf16[8192,512]{1,0:T(8,128)(2,1)} %wq_ref.1, bf16[8192,32]{1,0:T(8,128)(2,1)} %copy.14.wd_ref), custom_call_target="tpu_custom_call" | custom-call | tf_op jit(solution)/shard_map/project/pallas_call | solution.py:229
  39.1 0.0 copy-start
  39.1 2.4 %slice.9 = bf16[16,256,128]{2,1,0:T(8,128)(2,1)} slice(bf16[16,320,128]{2,1,0:T(8,128)(2,1)} %project.1), slice={[0:16], [0:256], [0:128]} | slice | bytes 2097152 | tf_op jit(solution)/shard_map/slice | solution.py:434
  41.5 1.0 slice_bitcast_fusion
  42.5 0.2 copy.15
  42.6 0.2 reshape.31
  42.9 0.8 pad.8.fresh_ref
  43.6 0.0 copy-done
  43.6 1.0 copy.16
  44.6 0.6 pad_add_fusion.where_ref
  45.3 26.5 %flash.1 = (bf16[16,16,16,128]{3,2,1,0:T(8,128)(2,1)}, f32[16,256,128]{2,1,0:T(8,128)}) custom-call(s32[16]{0:T(128)} %lengths_ref.1, s32[2]{0:T(128)} %pad_add_fusion.where_ref, bf16[16,16,16,128]{3,2,1,0:T(8,128)(2,1)} %bitcast.8, bf16[16,16,512]{2,1,0:T(8,128)(2,1)} %pad.8.fresh_ref, bf16[16,1024,512]{2,1,0:T(8,128)(2,1)} %cache_ref.1, ...), custom_call_target="tpu_custom_call" | custom-call | flops 6442450944 | bytes 16777216 | tf_op jit(solution)/shard_map/flash/pallas_call | solution.py:86
  71.8 0.0 copy-start.1
  71.8 2.2 %slice_reduce_fusion = f32[16,256]{1,0:T(8,128)S(1)} fusion(f32[16,256,128]{2,1,0:T(8,128)} %get-tuple-element.8), kind=kLoop, calls=%fused_computation | loop fusion | bytes 32768 | tf_op jit(solution)/shard_map/slice | solution.py:439
  74.0 0.1 reshape_squeeze.3
  74.2 0.1 reshape.33
  74.3 0.6 pad.9.l_ref
  74.9 0.0 copy-done.1
  74.9 0.1 broadcast_in_dim.2
  75.0 0.1 mul.18
  75.1 0.7 fusion.perm_ref
  75.8 32.9 %finish.1 = bf16[2,2,8192]{2,1,0:T(2,128)(2,1)} custom-call(bf16[16,256,128]{2,1,0:T(8,128)(2,1)} %bitcast.7, f32[16,8,128]{2,1,0:T(8,128)} %pad.9.l_ref, bf16[64,64]{1,0:T(8,128)(2,1)} %fusion.perm_ref, bf16[512,8192]{1,0:T(8,128)(2,1)} %wo_ref.1), custom_call_target="tpu_custom_call" | custom-call | tf_op jit(solution)/shard_map/finish/pallas_call | solution.py:411
  108.7 1.5 %copy.19 = bf16[2,2,8192]{2,1,0:T(2,128)(2,1)} copy(bf16[2,2,8192]{2,1,0:T(2,128)(2,1)} %finish.1) | data formatting | bytes 131072
  (3 shorter events, 0.1 us)
Async XLA Ops:
  39.1 4.5 %copy-start = (bf16[256,1024]{1,0:T(8,128)(2,1)S(1)}, bf16[256,1024]{1,0:T(8,128)(2,1)}, u32[]{:S(2)}) copy-start(bf16[256,1024]{1,0:T(8,128)(2,1)} %param.15) | copy-start | bytes 1572868
  71.8 3.1 %copy-start.1 = (s32[16]{0:T(128)S(1)}, s32[16]{0:T(128)}, u32[]{:S(2)}) copy-start(s32[16]{0:T(128)} %param.12) | copy-start | bytes 196

commit v3 on v2

--- a/solution.py
+++ b/solution.py
@@ -12,6 +12,7 @@
 HD = 128
 R = 16
 NEG = -1e30
+LOG2E = 1.4426950408889634
 BF = jnp.bfloat16
 F32 = jnp.float32
 
@@ -20,103 +21,116 @@
     return lax.dot_general(a, b, (((1,), (1,)), ((), ())), preferred_element_type=F32)
 
 
-def flash_kernel(hl, lengths_ref, where_ref, q_ref, fresh_ref, cache_ref, upk_ref, upv_ref,
+def flash_kernel(hl, lengths_ref, both_ref, fresh_ref, cache_ref, upk_ref, upv_ref,
                  o_ref, lse_ref, hi_ref, lo_ref, lat_ref):
-    ndevs, _, per, _ = q_ref.shape
-    rank = upk_ref.shape[1]
+    ndevs = both_ref.shape[0]
+    _, _, per, rank = hi_ref.shape
     rows = ndevs * per
     each = ndevs // KVH
-    positions = cache_ref.shape[1]
-    req = pl.program_id(0)
-
-    @pl.when(req == 0)
+    batch, positions, _ = cache_ref.shape
+    step = pl.program_id(0)
+    me = lax.axis_index("xfer")
+
+    @pl.when(step == 0)
     def _():
         for g in range(KVH):
-            qg = q_ref[g * each:(g + 1) * each].reshape(each * R * per, HD)
-            a = jnp.dot(qg, upk_ref[g * HD:(g + 1) * HD], preferred_element_type=F32)
-            a = a * (HD ** -0.5)
+            qg = both_ref[g * each:(g + 1) * each, :R * per].reshape(each * R * per, HD)
+            a = dot_nt(qg, upk_ref[:, g * HD:(g + 1) * HD])
+            a = a * (HD ** -0.5 * LOG2E)
             hi = a.astype(BF)
             lo = (a - hi.astype(F32)).astype(BF)
             hi_ref[g * each:(g + 1) * each] = hi.reshape(each, R, per, rank)
             lo_ref[g * each:(g + 1) * each] = lo.reshape(each, R, per, rank)
-
-    first = where_ref[0] * positions
-    seen = lengths_ref[req] - first
-    last = where_ref[0] == where_ref[1] - 1
-
-    qh = hi_ref[:, pl.ds(req, 1)].reshape(rows, rank)
-    ql = lo_ref[:, pl.ds(req, 1)].reshape(rows, rank)
-    key = cache_ref[0, :, :rank]
-    val = cache_ref[0, :, rank:]
-    s = dot_nt(qh, key) + dot_nt(ql, key)
-    pos = lax.broadcasted_iota(jnp.int32, s.shape, 1)
-    s = jnp.where(pos < seen, s, NEG)
-    fk = fresh_ref[0, :, :rank]
-    fv = fresh_ref[0, :, rank:]
-    n = dot_nt(qh, fk) + dot_nt(ql, fk)
-    row = lax.broadcasted_iota(jnp.int32, n.shape, 0) % per
-    col = lax.broadcasted_iota(jnp.int32, n.shape, 1)
-    rs, rt = row // (2 * hl), (row // hl) % 2
-    ok = (rs == col // 2) & (col % 2 <= rt) & last
-    n = jnp.where(ok, n, NEG)
-    top = jnp.maximum(jnp.max(s, axis=1, keepdims=True), jnp.max(n, axis=1, keepdims=True))
-    p = jnp.exp(s - top)
-    pn = jnp.exp(n - top)
-    total = jnp.sum(p, axis=1, keepdims=True) + jnp.sum(pn, axis=1, keepdims=True)
-    acc = jnp.dot(p.astype(BF), val, preferred_element_type=F32)
-    acc = acc + jnp.dot(pn.astype(BF), fv, preferred_element_type=F32)
-    lat_ref[:, pl.ds(req, 1)] = (acc / total).astype(BF).reshape(ndevs, 1, per, rank)
-    lse_ref[0] = jnp.broadcast_to(top + jnp.log(total), (rows, 128))
-
-    @pl.when(req == R - 1)
+        lse_ref[...] = jnp.zeros_like(lse_ref)
+
+    lane = lax.broadcasted_iota(jnp.int32, (rows, HD), 1)
+
+    def scores(req, keys):
+        qh = hi_ref[:, pl.ds(req, 1)].reshape(rows, rank)
+        ql = lo_ref[:, pl.ds(req, 1)].reshape(rows, rank)
+        return dot_nt(qh, keys) + dot_nt(ql, keys)
+
+    def weigh(s, vals):
+        top = jnp.max(s, axis=1, keepdims=True)
+        p = jnp.exp2(s - top)
+        total = jnp.sum(p, axis=1, keepdims=True)
+        acc = jnp.dot(p.astype(BF), vals, preferred_element_type=F32)
+        return acc / total, top + jnp.log2(total)
+
+    pos = lax.broadcasted_iota(jnp.int32, (rows, positions), 1)
+    lses = lse_ref[...].reshape(rows, HD)
+    ahead = scores(step * batch, cache_ref[0, :, :rank])
+    for b in range(batch):
+        req = step * batch + b
+        s = ahead
+        if b + 1 < batch:
+            ahead = scores(req + 1, cache_ref[b + 1, :, :rank])
+        s = jnp.where(pos < lengths_ref[req] - me * positions, s, NEG)
+        out, lse = weigh(s, cache_ref[b, :, rank:])
+        lat_ref[:, pl.ds(req, 1)] = out.astype(BF).reshape(ndevs, 1, per, rank)
+        lses = jnp.where(lane == req, lse, lses)
+    lse_ref[...] = lses.reshape(lse_ref.shape)
+
+    @pl.when(me // batch == step)
+    def _():
+        n = scores(me, fresh_ref[:, :rank])
+        row = lax.broadcasted_iota(jnp.int32, n.shape, 0) % per
+        col = lax.broadcasted_iota(jnp.int32, n.shape, 1)
+        rs, rt = row // (2 * hl), (row // hl) % 2
+        n = jnp.where((rs == col // 2) & (col % 2 <= rt), n, NEG)
+        near, near_lse = weigh(n, fresh_ref[:, rank:])
+        lses = lse_ref[...].reshape(rows, HD)
+        far_lse = jnp.sum(jnp.where(lane == me, lses, 0.0), axis=1, keepdims=True)
+        far = lat_ref[:, pl.ds(me, 1)].reshape(rows, rank).astype(F32)
+        top = jnp.maximum(near_lse, far_lse)
+        en, ef = jnp.exp2(near_lse - top), jnp.exp2(far_lse - top)
+        out = far + (en / (en + ef)) * (near - far)
+        lat_ref[:, pl.ds(me, 1)] = out.astype(BF).reshape(ndevs, 1, per, rank)
+        lse = top + jnp.log2(en + ef)
+        lse_ref[...] = jnp.where(lane == me, lse, lses).reshape(lse_ref.shape)
+
+    @pl.when(step == R // batch - 1)
     def _():
         for g in range(KVH):
             lg = lat_ref[g * each:(g + 1) * each].reshape(each * R * per, rank)
             o = jnp.dot(lg, upv_ref[:, g * HD:(g + 1) * HD], preferred_element_type=F32)
-            o_ref[g * each:(g + 1) * each] = o.astype(BF).reshape(each, R, per, HD)
-
-
-def flash(q, fresh, cache, lengths, upk, upv, mine, ndevs, hl):
-    _, _, per, _ = q.shape
+            o_ref[g * each:(g + 1) * each] = o.astype(BF).reshape(each, R * per, HD)
+
+
+def flash(both, fresh, cache, lengths, upk, upv, hl, per, batch=4):
+    ndevs = both.shape[0]
     rank = upv.shape[0]
     rows = ndevs * per
     positions = cache.shape[1]
-    where = jnp.stack([mine, jnp.full_like(mine, ndevs)]).astype(jnp.int32)
-    whole = lambda a: pl.BlockSpec(a.shape, lambda i, *_: (0,) * a.ndim)
+    whole = lambda shape: pl.BlockSpec(shape, lambda i, *_: (0,) * len(shape))
+    state = pltpu.VMEM((ndevs, R, per, rank), BF)
     return pl.pallas_call(
         functools.partial(flash_kernel, hl),
         out_shape=(
-            jax.ShapeDtypeStruct((ndevs, R, per, HD), BF),
-            jax.ShapeDtypeStruct((R, rows, 128), F32),
+            jax.ShapeDtypeStruct((ndevs, R * per, HD), BF),
+            jax.ShapeDtypeStruct((ndevs, per, HD), F32),
         ),
         grid_spec=pltpu.PrefetchScalarGridSpec(
-            num_scalar_prefetch=2,
-            grid=(R,),
+            num_scalar_prefetch=1,
+            grid=(R // batch,),
             in_specs=[
-                whole(q),
-                pl.BlockSpec((1,) + fresh.shape[1:], lambda i, *_: (i, 0, 0)),
-                pl.BlockSpec((1, positions, 2 * rank), lambda i, *_: (i, 0, 0)),
-                whole(upk),
-                whole(upv),
+                whole(both.shape),
+                whole(fresh.shape),
+                pl.BlockSpec((batch, positions, 2 * rank), lambda i, *_: (i, 0, 0)),
+                whole(upk.shape),
+                whole(upv.shape),
             ],
-            out_specs=[
-                pl.BlockSpec((ndevs, R, per, HD), lambda i, *_: (0, 0, 0, 0)),
-                pl.BlockSpec((1, rows, 128), lambda i, *_: (i, 0, 0)),
-            ],
-            scratch_shapes=[
-                pltpu.VMEM((ndevs, R, per, rank), BF),
-                pltpu.VMEM((ndevs, R, per, rank), BF),
-                pltpu.VMEM((ndevs, R, per, rank), BF),
-            ],
+            out_specs=[whole((ndevs, R * per, HD)), whole((ndevs, per, HD))],
+            scratch_shapes=[state, state, state],
         ),
-        compiler_params=pltpu.CompilerParams(vmem_limit_bytes=56 * 2 ** 20),
+        compiler_params=pltpu.CompilerParams(vmem_limit_bytes=60 * 2 ** 20),
         cost_estimate=pl.CostEstimate(
             flops=2 * R * rows * positions * rank * 3,
             bytes_accessed=cache.size * 2,
             transcendentals=R * rows * positions,
         ),
         name="flash",
-    )(lengths, where, q, fresh, cache, upk, upv)
+    )(lengths, both, fresh, cache, upk, upv)
 
 
 def place(ndevs):
@@ -192,7 +206,7 @@
     tiles = width // HD
     nrows = ndevs * slots * 2
     hl = wqv_ref.shape[1] // HD
-    fw = wdv_ref.shape[1]
+    fw = wdv_ref.shape[0]
     for s in range(slots):
         for t in range(tiles):
             wide_ref[pl.ds(s * 2 * tiles + t, 2, stride=tiles), :] = (
@@ -211,7 +225,7 @@
             [wide_ref[pl.ds(t + i, nrows, stride=tiles), :].astype(BF) for i in range(step)], axis=1)
         span = slice(t * HD, (t + step) * HD)
         query = query + jnp.dot(xt, wqv_ref[span], preferred_element_type=F32)
-        fresh = fresh + jnp.dot(xt, wdv_ref[span], preferred_element_type=F32)
+        fresh = fresh + dot_nt(xt, wdv_ref[:, span])
     for h in range(hl):
         stage_ref[pl.ds(h, nrows, stride=hl), :] = query[:, h * HD:(h + 1) * HD]
     stage_ref[nrows * hl:, :] = jnp.zeros((nrows, HD), F32)
@@ -302,30 +316,32 @@
             copy.wait_send()
 
 
-def turn(w):
-    return jnp.transpose(jnp.broadcast_to(w, (HD, HD)))
+def weighted(terms):
+    per = terms[0][0].shape[0]
+    for req in range(R):
+        span = slice(req * per, (req + 1) * per)
+        got = None
+        for share, block in terms:
+            term = share[:, req:req + 1] * block[span].astype(F32)
+            got = term if got is None else got + term
+        yield span, got
 
 
 def merge_heads(dst, a, b):
-    n = a[0].shape[0] // HD
     la, lb = a[1][...], b[1][...]
     top = jnp.maximum(la, lb)
-    ea, eb = jnp.exp(la - top), jnp.exp(lb - top)
+    ea, eb = jnp.exp2(la - top), jnp.exp2(lb - top)
     both = ea + eb
-    share = ea / both
-    lse = top + jnp.log(both)
-    for t in range(n):
-        span = slice(t * HD, (t + 1) * HD)
-        oa, ob = a[0][span].astype(F32), b[0][span].astype(F32)
-        dst[0][span] = (ob + turn(share[t:t + 1]) * (oa - ob)).astype(BF)
-    dst[1][...] = lse
+    for span, got in weighted([(ea / both, a[0]), (eb / both, b[0])]):
+        dst[0][span] = got.astype(BF)
+    dst[1][...] = top + jnp.log2(both)
 
 
 def merge_sums(dst, a, b):
     dst[0][...] = (a[0][...].astype(F32) + b[0][...].astype(F32)).astype(BF)
 
 
-def finish_kernel(ndevs, o_ref, l_ref, perm_ref, wo_ref, out_ref,
+def finish_kernel(ndevs, o_ref, l_ref, place_ref, wo_ref, out_ref,
                   ob_ref, lb_ref, o1, l1, o2, l2, o3, l3, wov_ref, head_ref, wide_ref, *rest):
     pieces = (len(rest) - 3) // 4
     sums = rest[:4 * pieces]
@@ -345,23 +361,26 @@
     greet(ndevs)
 
     def finish_heads(mine, others):
-        n = mine[0].shape[0] // HD
         ls = [mine[1][...]] + [o[1][...] for o in others]
         top = functools.reduce(jnp.maximum, ls)
-        es = [jnp.exp(l - top) for l in ls]
+        es = [jnp.exp2(l - top) for l in ls]
         both = functools.reduce(jnp.add, es)
-        for t in range(n):
-            span = slice(t * HD, (t + 1) * HD)
-            got = jnp.zeros((HD, HD), F32)
-            for e, o in zip(es, [mine] + list(others)):
-                got = got + turn((e / both)[t:t + 1]) * o[0][span].astype(F32)
+        refs = [mine[0]] + [o[0] for o in others]
+        for span, got in weighted([(e / both, r) for e, r in zip(es, refs)]):
             head_ref[span] = got
 
     fold(ndevs, (ob_ref, lb_ref), (o1, l1), (o2, l2), (o3, l3),
          send.at[0], recv.at[0], merge_heads, finish_heads)
     heads = [head_ref[pl.ds(h, nrows, stride=hl), :].astype(BF) for h in range(hl)]
     head = jnp.concatenate(heads, axis=1)
-    head = jnp.dot(perm_ref[...], head, preferred_element_type=F32).astype(BF)
+    row = lax.broadcasted_iota(jnp.int32, (nrows, nrows), 0)
+    col = lax.broadcasted_iota(jnp.int32, (nrows, nrows), 1)
+    block = nrows // R
+    source = row % block
+    for j in range(R):
+        source = source + jnp.where(row // block == j, place_ref[j] * block, 0)
+    perm = jnp.where(col == source, 1.0, 0.0).astype(BF)
+    head = jnp.dot(perm, head, preferred_element_type=F32).astype(BF)
     for copy in copies:
         copy.wait()
     for p in range(pieces):
@@ -389,7 +408,7 @@
              send.at[1 + p], recv.at[1 + p], merge_sums, finish_sums)
 
 
-def finish(o, lse, perm, wo, ndevs, slots, pieces=1):
+def finish(o, lse, placement, wo, ndevs, slots, pieces=1):
     width = wo.shape[1]
     deep = ndevs // 4
     rows = o.shape[1]
@@ -411,18 +430,22 @@
     return pl.pallas_call(
         functools.partial(finish_kernel, ndevs),
         out_shape=jax.ShapeDtypeStruct((slots, 2, width), BF),
-        in_specs=[pl.BlockSpec(memory_space=pltpu.VMEM)] * 3 + [pl.BlockSpec(memory_space=pl.ANY)],
+        in_specs=[
+            pl.BlockSpec(memory_space=pltpu.VMEM),
+            pl.BlockSpec(memory_space=pltpu.VMEM),
+            pl.BlockSpec(memory_space=pltpu.SMEM),
+            pl.BlockSpec(memory_space=pl.ANY),
+        ],
         out_specs=pl.BlockSpec(memory_space=pltpu.VMEM),
         scratch_shapes=scratch,
         compiler_params=pltpu.CompilerParams(
             collective_id=1, has_side_effects=True, vmem_limit_bytes=56 * 2 ** 20),
         name="finish",
-    )(o, lse, perm, wo)
+    )(o, lse, placement, wo)
 
 
 def local(hidden_in, latent_cache, lengths, placement, w_query, w_down, up_key, up_value, w_out):
     ndevs = lax.axis_size("xfer")
-    mine = lax.axis_index("xfer")
     rank = up_key.shape[0]
     hl = w_query.shape[1] // HD
     fw = w_down.shape[1]
@@ -430,18 +453,14 @@
     samples = slot_rows * ndevs // R
     nrows = slot_rows * 2 * ndevs
     per = samples * 2 * hl
-    both = project(hidden_in, w_query, w_down, ndevs)
-    q = both[:, :nrows * hl].reshape(ndevs, R, per, HD)
-    own = both[:, nrows * hl:, :fw].transpose(1, 0, 2).reshape(R, samples * 2, 2 * rank)
-    pad = -(samples * 2) % 16
-    own = jnp.pad(own, ((0, 0), (0, pad), (0, 0)))
-    o, lse = flash(q, own, latent_cache, lengths, up_key.T, up_value, mine, ndevs, hl)
-    lse = lse[:, :, 0].reshape(R, ndevs, per).transpose(1, 0, 2).reshape(ndevs, R * per // HD, HD)
-    lse = jnp.pad(lse, ((0, 0), (0, 8 - R * per // HD), (0, 0)))
-    slot = jnp.arange(nrows, dtype=jnp.int32)
-    source = jnp.repeat(placement, 2 * samples) * (2 * samples) + slot % (2 * samples)
-    perm = (source[:, None] == slot[None, :]).astype(BF)
-    return finish(o.reshape(ndevs, R * per, HD), lse, perm, w_out, ndevs, slot_rows)
+    both = project(hidden_in, w_query, w_down.T, ndevs)
+    near = samples * 2
+    request = jnp.minimum(lax.axis_index("xfer"), R - 1)
+    own = lax.dynamic_slice_in_dim(both, nrows * hl + request * near, near, 1)[:, :, :fw]
+    own = own.transpose(1, 0, 2).reshape(near, 2 * rank)
+    own = jnp.pad(own, ((0, -near % 16), (0, 0)))
+    o, lse = flash(both, own, latent_cache, lengths, up_key, up_value, hl, per)
+    return finish(o, lse, placement, w_out, ndevs, slot_rows)
 
 
 def solution(mesh):

time: 111 us -> 89.1 us (0.80)
  Pallas kernels: 95.8 us -> 85.8 us
  local copies, waits for them, and re-layouts: 13 us -> 3 us
  other arithmetic: 1.33 us -> 0 us
    pallas_call x1, Pallas kernels: 26.5 us -> 16.2 us  [flash(): pl.pallas_call(functools.partial(flash_kernel, hl), out_shape=(jax.ShapeD...]
    slice x2 -> x0, local copies, waits for them, and re-layouts: 4.61 us -> none  [the longest x1 2.4 us: local(): q = both[:, :nrows * hl].reshape(ndevs, R, per, HD)]
    unnamed x7 -> x1, local copies, waits for them, and re-layouts: 5.22 us -> 1.52 us
where the time goes in v3:
time: 89.1 us; the launch traced here: 88.8 us
  Pallas kernels  85.8 us (96%)
  local copies, waits for them, and re-layouts  3 us (3%)
    pallas_call x1, Pallas kernels, project(): pl.pallas_call(functools.partial(project_kernel, ndevs), out_shape=jax.Sh...  36.5 us
    pallas_call x1, Pallas kernels, finish(): pl.pallas_call(functools.partial(finish_kernel, ndevs), out_shape=jax.Sha...  33.2 us
    pallas_call x1, Pallas kernels, flash(): pl.pallas_call(functools.partial(flash_kernel, hl), out_shape=(jax.ShapeD...  16.2 us

profile of v3, /device:TPU:0, one launch (start us, length us, event | category | flops | bytes accessed | tf_op | source)
XLA Modules:
  0.0 88.8 jit_solution(8037667891508630011)
XLA Ops:
  0.0 36.5 %project.1.both_ref = bf16[16,320,128]{2,1,0:T(8,128)(2,1)} custom-call(bf16[2,2,8192]{2,1,0:T(2,128)(2,1)} %hidden_ref.1, bf16[8192,512]{1,0:T(8,128)(2,1)} %wq_ref.1, bf16[32,8192]{1,0:T(8,128)(2,1)} %bitcast.3), custom_call_target="tpu_custom_call" | custom-call | tf_op jit(solution)/shard_map/project/pallas_call | solution.py:243
  36.5 0.8 dynamic-slice_bitcast_fusion
  37.3 0.1 reshape.3
  37.3 0.6 pad.4.fresh_ref
  38.0 16.2 %flash.1 = (bf16[16,256,128]{2,1,0:T(8,128)(2,1)}, f32[16,16,128]{2,1,0:T(8,128)}) custom-call(s32[16]{0:T(128)} %lengths_ref.1, bf16[16,320,128]{2,1,0:T(8,128)(2,1)} %project.1.both_ref, bf16[16,512]{1,0:T(8,128)(2,1)} %pad.4.fresh_ref, bf16[16,1024,512]{2,1,0:T(8,128)(2,1)} %cache_ref.1, bf16[256,1024]{1,0:T(8,128)(2,1)} %upk_ref.1, bf16[256,1024]{1,0:T(8,128)(2,1)} %upv_ref.1), custom_call_target="tpu_custom_call" | custom-call | flops 6442450944 | bytes 16777216 | tf_op jit(solution)/shard_map/flash/pallas_call | solution.py:107
  54.1 33.2 %finish.1 = bf16[2,2,8192]{2,1,0:T(2,128)(2,1)} custom-call(bf16[16,256,128]{2,1,0:T(8,128)(2,1)} %get-tuple-element.7.o_ref, f32[16,16,128]{2,1,0:T(8,128)} %get-tuple-element.8.l_ref, s32[16]{0:T(128)} %place_ref.1, bf16[512,8192]{1,0:T(8,128)(2,1)} %wo_ref.1), custom_call_target="tpu_custom_call" | custom-call | tf_op jit(solution)/shard_map/finish/pallas_call | solution.py:430
  87.3 1.5 %copy.12 = bf16[2,2,8192]{2,1,0:T(2,128)(2,1)} copy(bf16[2,2,8192]{2,1,0:T(2,128)(2,1)} %finish.1) | data formatting | bytes 131072
  (1 shorter events, 0.0 us)

commit v4 on v3

--- a/solution.py
+++ b/solution.py
@@ -174,6 +174,8 @@
         copy.start()
     across, over = [], []
     for k in range(deep + 1):
+        if k:
+            yield
         if k < deep:
             block = index_of((z - k + deep) % deep, y, c)
             if k:
@@ -187,14 +189,23 @@
             block = index_of((z - k + 1 + deep) % deep, 1 - y, c)
             over.append(move(block, twin + deep + k - 1, index_of(z, y, 1 - c)))
             over[-1].start()
+    yield
     for copy in over:
         copy.wait_recv()
     for copy in along + across + over:
         copy.wait_send()
 
 
+def drive(*works):
+    works = list(works)
+    while works:
+        for work in list(works):
+            if next(work, works) is works:
+                works.remove(work)
+
+
 def project_kernel(ndevs, hidden_ref, wq_ref, wd_ref, out_ref,
-                   x_ref, wide_ref, wqv_ref, wdv_ref, stage_ref, send, recv, send2, recv2, wsem):
+                   x_ref, wide_ref, wqv_ref, wdv_ref, stage_ref, send, recv, wsem):
     copies = [
         pltpu.make_async_copy(wq_ref, wqv_ref, wsem.at[0]),
         pltpu.make_async_copy(wd_ref, wdv_ref, wsem.at[1]),
@@ -203,46 +214,57 @@
         copy.start()
     me = lax.axis_index("xfer")
     slots, _, width = hidden_ref.shape
-    tiles = width // HD
+    pieces = x_ref.shape[0]
+    tiles = width // HD // pieces
     nrows = ndevs * slots * 2
     hl = wqv_ref.shape[1] // HD
     fw = wdv_ref.shape[0]
-    for s in range(slots):
-        for t in range(tiles):
-            wide_ref[pl.ds(s * 2 * tiles + t, 2, stride=tiles), :] = (
-                hidden_ref[s, :, t * HD:(t + 1) * HD].astype(F32))
-    x_ref[pl.ds(me, 1)] = wide_ref[:slots * 2 * tiles, :].astype(BF)[None]
+    for p in range(pieces):
+        for s in range(slots):
+            for t in range(tiles):
+                at = (p * tiles + t) * HD
+                wide_ref[pl.ds(s * 2 * tiles + t, 2, stride=tiles), :] = (
+                    hidden_ref[s, :, at:at + HD].astype(F32))
+        x_ref[p, pl.ds(me, 1)] = wide_ref[:slots * 2 * tiles, :].astype(BF)[None]
     greet(ndevs)
-    spread(ndevs, x_ref, send, recv)
-    wide_ref[...] = x_ref[...].astype(F32).reshape(wide_ref.shape)
+    sums = [jnp.zeros((nrows, hl * HD), F32), jnp.zeros((nrows, fw), F32)]
+
+    def multiply(p, step=8):
+        wide_ref[...] = x_ref[p].astype(F32).reshape(wide_ref.shape)
+        for t in range(0, tiles, step):
+            xt = jnp.concatenate(
+                [wide_ref[pl.ds(t + i, nrows, stride=tiles), :].astype(BF) for i in range(step)], axis=1)
+            span = slice((p * tiles + t) * HD, (p * tiles + t + step) * HD)
+            sums[0] = sums[0] + jnp.dot(xt, wqv_ref[span], preferred_element_type=F32)
+            sums[1] = sums[1] + dot_nt(xt, wdv_ref[:, span])
+            yield
+
+    gathers = [spread(ndevs, x_ref.at[p], send.at[p], recv.at[p]) for p in range(pieces)]
+    for gather in gathers:
+        next(gather)
+    drive(gathers[0])
     for copy in copies:
         copy.wait()
-    query = jnp.zeros((nrows, hl * HD), F32)
-    fresh = jnp.zeros((nrows, fw), F32)
-    step = 16
-    for t in range(0, tiles, step):
-        xt = jnp.concatenate(
-            [wide_ref[pl.ds(t + i, nrows, stride=tiles), :].astype(BF) for i in range(step)], axis=1)
-        span = slice(t * HD, (t + step) * HD)
-        query = query + jnp.dot(xt, wqv_ref[span], preferred_element_type=F32)
-        fresh = fresh + dot_nt(xt, wdv_ref[:, span])
+    for p in range(pieces):
+        drive(*gathers[p + 1:p + 2], multiply(p))
+    query, fresh = sums
     for h in range(hl):
         stage_ref[pl.ds(h, nrows, stride=hl), :] = query[:, h * HD:(h + 1) * HD]
-    stage_ref[nrows * hl:, :] = jnp.zeros((nrows, HD), F32)
-    stage_ref[nrows * hl:, :fw] = fresh
+    for i in range(nrows // 16):
+        stage_ref[nrows * hl:, i * fw:(i + 1) * fw] = fresh[i * 16:(i + 1) * 16]
     out_ref[pl.ds(me, 1)] = stage_ref[...].astype(BF)[None]
-    spread(ndevs, out_ref, send2, recv2)
-
-
-def project(hidden, wq, wd, ndevs):
+    drive(spread(ndevs, out_ref, send.at[pieces], recv.at[pieces]))
+
+
+def project(hidden, wq, wd, ndevs, pieces=2):
     slots, _, width = hidden.shape
-    tall = slots * 2 * width // HD
+    tall = slots * 2 * width // HD // pieces
     nrows = ndevs * slots * 2
     hl = wq.shape[1] // HD
-    sems = pltpu.SemaphoreType.DMA((ndevs,))
+    sems = pltpu.SemaphoreType.DMA((pieces + 1, ndevs))
     return pl.pallas_call(
         functools.partial(project_kernel, ndevs),
-        out_shape=jax.ShapeDtypeStruct((ndevs, nrows * (hl + 1), HD), BF),
+        out_shape=jax.ShapeDtypeStruct((ndevs, nrows * hl + 16, HD), BF),
         in_specs=[
             pl.BlockSpec(memory_space=pltpu.VMEM),
             pl.BlockSpec(memory_space=pl.ANY),
@@ -250,12 +272,12 @@
         ],
         out_specs=pl.BlockSpec(memory_space=pltpu.VMEM),
         scratch_shapes=[
-            pltpu.VMEM((ndevs, tall, HD), BF),
+            pltpu.VMEM((pieces, ndevs, tall, HD), BF),
             pltpu.VMEM((ndevs * tall, HD), F32),
             pltpu.VMEM(wq.shape, BF),
             pltpu.VMEM(wd.shape, BF),
-            pltpu.VMEM((nrows * (hl + 1), HD), F32),
-            sems, sems, sems, sems,
+            pltpu.VMEM((nrows * hl + 16, HD), F32),
+            sems, sems,
             pltpu.SemaphoreType.DMA((2,)),
         ],
         compiler_params=pltpu.CompilerParams(
@@ -293,21 +315,25 @@
             first.append(ship(at(blocks, index_of(order[k], yy, 1 - c)), at(held1, far * deep + k), twin))
     second = []
     for k in range(deep):
+        yield
         arrive(first[k])
         here = at(blocks, index_of(order[k], 1 - y, c))
         merge(here, here, at(held1, deep + k))
         second.append(ship(here, at(held2, k), index_of(z, 1 - y, c)))
     for k in range(deep):
+        yield
         arrive(first[deep + k])
         here = at(blocks, index_of(order[k], y, c))
         merge(here, here, at(held1, k))
     third = []
     for k in range(deep):
+        yield
         arrive(second[k])
         here = at(blocks, index_of(order[k], y, c))
         merge(here, here, at(held2, k))
         if k < deep - 1:
             third.append(ship(here, at(held3, k), index_of(order[k], y, c)))
+    yield
     for copies in third:
         arrive(copies)
     finish(at(blocks, index_of(z, y, c)), [at(held3, k) for k in range(deep - 1)])
@@ -342,12 +368,14 @@
 
 
 def finish_kernel(ndevs, o_ref, l_ref, place_ref, wo_ref, out_ref,
-                  ob_ref, lb_ref, o1, l1, o2, l2, o3, l3, wov_ref, head_ref, wide_ref, *rest):
+                  ob_ref, lb_ref, o1, l1, o2, l2, o3, l3, wov_ref, head_ref, wide_ref, small_ref, *rest):
     pieces = (len(rest) - 3) // 4
     sums = rest[:4 * pieces]
     send, recv, wsem = rest[-3:]
     copies = [
-        pltpu.make_async_copy(wo_ref, wov_ref, wsem.at[0]),
+        pltpu.make_async_copy(o_ref, ob_ref, wsem.at[0]),
+        pltpu.make_async_copy(l_ref, lb_ref, wsem.at[1]),
+        pltpu.make_async_copy(wo_ref, wov_ref, wsem.at[2]),
     ]
     for copy in copies:
         copy.start()
@@ -356,9 +384,9 @@
     nrows = ndevs * slots * 2
     hl = wov_ref.shape[0] // HD
     tiles = width // HD // pieces
-    ob_ref[...] = o_ref[...]
-    lb_ref[...] = l_ref[...]
     greet(ndevs)
+    for copy in copies[:2]:
+        copy.wait()
 
     def finish_heads(mine, others):
         ls = [mine[1][...]] + [o[1][...] for o in others]
@@ -369,8 +397,8 @@
         for span, got in weighted([(e / both, r) for e, r in zip(es, refs)]):
             head_ref[span] = got
 
-    fold(ndevs, (ob_ref, lb_ref), (o1, l1), (o2, l2), (o3, l3),
-         send.at[0], recv.at[0], merge_heads, finish_heads)
+    drive(fold(ndevs, (ob_ref, lb_ref), (o1, l1), (o2, l2), (o3, l3),
+               send.at[0], recv.at[0], merge_heads, finish_heads))
     heads = [head_ref[pl.ds(h, nrows, stride=hl), :].astype(BF) for h in range(hl)]
     head = jnp.concatenate(heads, axis=1)
     row = lax.broadcasted_iota(jnp.int32, (nrows, nrows), 0)
@@ -381,34 +409,41 @@
         source = source + jnp.where(row // block == j, place_ref[j] * block, 0)
     perm = jnp.where(col == source, 1.0, 0.0).astype(BF)
     head = jnp.dot(perm, head, preferred_element_type=F32).astype(BF)
-    for copy in copies:
-        copy.wait()
-    for p in range(pieces):
-        step = 8
+    copies[2].wait()
+
+    def multiply(p, step=8):
         for t in range(0, tiles, step):
             at = (p * tiles + t) * HD
             got = jnp.dot(head, wov_ref[:, at:at + step * HD], preferred_element_type=F32)
             for i in range(step):
                 wide_ref[pl.ds(t + i, nrows, stride=tiles), :] = got[:, i * HD:(i + 1) * HD]
-        buf = sums[4 * p]
-        buf[...] = wide_ref[...].astype(BF).reshape(buf.shape)
-
-        def finish_sums(mine, others, p=p):
-            total = mine[0][...].astype(F32)
-            for o in others:
-                total = total + o[0][...].astype(F32)
-            wide_ref[:slots * 2 * tiles, :] = total
-            for s in range(slots):
-                for t in range(tiles):
-                    at = (p * tiles + t) * HD
-                    out_ref[s, :, at:at + HD] = (
-                        wide_ref[pl.ds(s * 2 * tiles + t, 2, stride=tiles), :].astype(BF))
-
-        fold(ndevs, (buf,), (sums[4 * p + 1],), (sums[4 * p + 2],), (sums[4 * p + 3],),
-             send.at[1 + p], recv.at[1 + p], merge_sums, finish_sums)
-
-
-def finish(o, lse, placement, wo, ndevs, slots, pieces=1):
+            yield
+        sums[4 * p][...] = wide_ref[...].astype(BF).reshape(sums[4 * p].shape)
+
+    def finish_sums(p, mine, others):
+        total = mine[0][...].astype(F32)
+        for o in others:
+            total = total + o[0][...].astype(F32)
+        small_ref[...] = total
+        for s in range(slots):
+            for t in range(tiles):
+                at = (p * tiles + t) * HD
+                out_ref[s, :, at:at + HD] = (
+                    small_ref[pl.ds(s * 2 * tiles + t, 2, stride=tiles), :].astype(BF))
+
+    folds = []
+    for p in range(pieces):
+        for _ in multiply(p):
+            if folds:
+                next(folds[-1])
+        refs = sums[4 * p:4 * p + 4]
+        folds.append(fold(ndevs, refs[:1], refs[1:2], refs[2:3], refs[3:],
+                          send.at[1 + p], recv.at[1 + p], merge_sums, functools.partial(finish_sums, p)))
+        next(folds[-1])
+    drive(*folds)
+
+
+def finish(o, lse, placement, wo, ndevs, slots, pieces=2):
     width = wo.shape[1]
     deep = ndevs // 4
     rows = o.shape[1]
@@ -422,17 +457,18 @@
         pltpu.VMEM(wo.shape, BF),
         pltpu.VMEM((rows, HD), F32),
         pltpu.VMEM((ndevs * tall, HD), F32),
+        pltpu.VMEM((tall, HD), F32),
     ]
     for _ in range(pieces):
         scratch += [pltpu.VMEM((n, tall, HD), BF) for n in sizes]
     sems = pltpu.SemaphoreType.DMA((1 + pieces, 8 * deep))
-    scratch += [sems, sems, pltpu.SemaphoreType.DMA((1,))]
+    scratch += [sems, sems, pltpu.SemaphoreType.DMA((3,))]
     return pl.pallas_call(
         functools.partial(finish_kernel, ndevs),
         out_shape=jax.ShapeDtypeStruct((slots, 2, width), BF),
         in_specs=[
-            pl.BlockSpec(memory_space=pltpu.VMEM),
-            pl.BlockSpec(memory_space=pltpu.VMEM),
+            pl.BlockSpec(memory_space=pl.ANY),
+            pl.BlockSpec(memory_space=pl.ANY),
             pl.BlockSpec(memory_space=pltpu.SMEM),
             pl.BlockSpec(memory_space=pl.ANY),
         ],
@@ -456,7 +492,9 @@
     both = project(hidden_in, w_query, w_down.T, ndevs)
     near = samples * 2
     request = jnp.minimum(lax.axis_index("xfer"), R - 1)
-    own = lax.dynamic_slice_in_dim(both, nrows * hl + request * near, near, 1)[:, :, :fw]
+    row = request * near
+    own = lax.dynamic_slice(
+        both, (0, nrows * hl + row % 16, row // 16 * fw), (ndevs, near, fw))
     own = own.transpose(1, 0, 2).reshape(near, 2 * rank)
     own = jnp.pad(own, ((0, -near % 16), (0, 0)))
     o, lse = flash(both, own, latent_cache, lengths, up_key, up_value, hl, per)

time: 89.1 us -> 94.4 us (1.059)
  Pallas kernels: 85.8 us -> 91 us
    pallas_call x1, Pallas kernels: 36.5 us -> 40.1 us  [project(): pl.pallas_call(functools.partial(project_kernel, ndevs), out_shape=jax.Sh...]
    pallas_call x1, Pallas kernels: 33.2 us -> 34.5 us  [finish(): pl.pallas_call(functools.partial(finish_kernel, ndevs), out_shape=jax.Sha...]
where the time goes in v4:
time: 94.4 us; the launch traced here: 94.1 us
  Pallas kernels  91 us (96%)
  local copies, waits for them, and re-layouts  3.08 us (3%)
    pallas_call x1, Pallas kernels, project(): pl.pallas_call(functools.partial(project_kernel, ndevs), out_shape=jax.Sh...  40.1 us
    pallas_call x1, Pallas kernels, finish(): pl.pallas_call(functools.partial(finish_kernel, ndevs), out_shape=jax.Sha...  34.5 us
    pallas_call x1, Pallas kernels, flash(): pl.pallas_call(functools.partial(flash_kernel, hl), out_shape=(jax.ShapeD...  16.3 us

profile of v4, /device:TPU:0, one launch (start us, length us, event | category | flops | bytes accessed | tf_op | source)
XLA Modules:
  0.0 94.1 jit_solution(6040924289831881465)
XLA Ops:
  0.0 40.1 %project.1.both_ref = bf16[16,272,128]{2,1,0:T(8,128)(2,1)} custom-call(bf16[2,2,8192]{2,1,0:T(2,128)(2,1)} %hidden_ref.1, bf16[8192,512]{1,0:T(8,128)(2,1)} %wq_ref.1, bf16[32,8192]{1,0:T(8,128)(2,1)} %bitcast.3), custom_call_target="tpu_custom_call" | custom-call | tf_op jit(solution)/shard_map/project/pallas_call | solution.py:265
  40.1 0.8 dynamic-slice_bitcast_fusion
  41.0 0.1 reshape.3
  41.1 0.6 pad.4.fresh_ref
  41.7 16.3 %flash.1 = (bf16[16,256,128]{2,1,0:T(8,128)(2,1)}, f32[16,16,128]{2,1,0:T(8,128)}) custom-call(s32[16]{0:T(128)} %lengths_ref.1, bf16[16,272,128]{2,1,0:T(8,128)(2,1)} %project.1.both_ref, bf16[16,512]{1,0:T(8,128)(2,1)} %pad.4.fresh_ref, bf16[16,1024,512]{2,1,0:T(8,128)(2,1)} %cache_ref.1, bf16[256,1024]{1,0:T(8,128)(2,1)} %upk_ref.1, bf16[256,1024]{1,0:T(8,128)(2,1)} %upv_ref.1), custom_call_target="tpu_custom_call" | custom-call | flops 6442450944 | bytes 16777216 | tf_op jit(solution)/shard_map/flash/pallas_call | solution.py:107
  58.0 34.5 %finish.1 = bf16[2,2,8192]{2,1,0:T(2,128)(2,1)} custom-call(bf16[16,256,128]{2,1,0:T(8,128)(2,1)} %get-tuple-element.7.o_ref, f32[16,16,128]{2,1,0:T(8,128)} %get-tuple-element.8.l_ref, s32[16]{0:T(128)} %place_ref.1, bf16[512,8192]{1,0:T(8,128)(2,1)} %wo_ref.1), custom_call_target="tpu_custom_call" | custom-call | tf_op jit(solution)/shard_map/finish/pallas_call | solution.py:466
  92.5 1.5 %copy.12 = bf16[2,2,8192]{2,1,0:T(2,128)(2,1)} copy(bf16[2,2,8192]{2,1,0:T(2,128)(2,1)} %finish.1) | data formatting | bytes 131072
  (1 shorter events, 0.0 us)

commit v5 on v4

--- a/solution.py
+++ b/solution.py
@@ -48,7 +48,7 @@
     def scores(req, keys):
         qh = hi_ref[:, pl.ds(req, 1)].reshape(rows, rank)
         ql = lo_ref[:, pl.ds(req, 1)].reshape(rows, rank)
-        return dot_nt(qh, keys) + dot_nt(ql, keys)
+        return dot_nt(jnp.concatenate([qh, ql], axis=1), jnp.concatenate([keys, keys], axis=1))
 
     def weigh(s, vals):
         top = jnp.max(s, axis=1, keepdims=True)
@@ -229,7 +229,7 @@
     greet(ndevs)
     sums = [jnp.zeros((nrows, hl * HD), F32), jnp.zeros((nrows, fw), F32)]
 
-    def multiply(p, step=8):
+    def multiply(p, step=16):
         wide_ref[...] = x_ref[p].astype(F32).reshape(wide_ref.shape)
         for t in range(0, tiles, step):
             xt = jnp.concatenate(
@@ -256,7 +256,7 @@
     drive(spread(ndevs, out_ref, send.at[pieces], recv.at[pieces]))
 
 
-def project(hidden, wq, wd, ndevs, pieces=2):
+def project(hidden, wq, wd, ndevs, pieces=1):
     slots, _, width = hidden.shape
     tall = slots * 2 * width // HD // pieces
     nrows = ndevs * slots * 2
@@ -429,7 +429,7 @@
             for t in range(tiles):
                 at = (p * tiles + t) * HD
                 out_ref[s, :, at:at + HD] = (
-                    small_ref[pl.ds(s * 2 * tiles + t, 2, stride=tiles), :].astype(BF))
+                    small_ref[pl.ds(s * 2 * tiles + t, 2, stride=tiles), :])
 
     folds = []
     for p in range(pieces):
@@ -443,7 +443,7 @@
     drive(*folds)
 
 
-def finish(o, lse, placement, wo, ndevs, slots, pieces=2):
+def finish(o, lse, placement, wo, ndevs, slots, pieces=1):
     width = wo.shape[1]
     deep = ndevs // 4
     rows = o.shape[1]
@@ -465,7 +465,7 @@
     scratch += [sems, sems, pltpu.SemaphoreType.DMA((3,))]
     return pl.pallas_call(
         functools.partial(finish_kernel, ndevs),
-        out_shape=jax.ShapeDtypeStruct((slots, 2, width), BF),
+        out_shape=jax.ShapeDtypeStruct((slots, 2, width), F32),
         in_specs=[
             pl.BlockSpec(memory_space=pl.ANY),
             pl.BlockSpec(memory_space=pl.ANY),
@@ -496,9 +496,8 @@
     own = lax.dynamic_slice(
         both, (0, nrows * hl + row % 16, row // 16 * fw), (ndevs, near, fw))
     own = own.transpose(1, 0, 2).reshape(near, 2 * rank)
-    own = jnp.pad(own, ((0, -near % 16), (0, 0)))
     o, lse = flash(both, own, latent_cache, lengths, up_key, up_value, hl, per)
-    return finish(o, lse, placement, w_out, ndevs, slot_rows)
+    return finish(o, lse, placement, w_out, ndevs, slot_rows).astype(BF)
 
 
 def solution(mesh):

time: 94.4 us -> 87.3 us (0.925)
  Pallas kernels: 91 us -> 83.9 us
  other arithmetic: 0 us -> 1.58 us
  local copies, waits for them, and re-layouts: 3.08 us -> 1.54 us
    pallas_call x1, Pallas kernels: 40.1 us -> 35.3 us  [project(): pl.pallas_call(functools.partial(project_kernel, ndevs), out_shape=jax.Sh...]
    pallas_call x1, Pallas kernels: 34.5 us -> 32.6 us  [finish(): pl.pallas_call(functools.partial(finish_kernel, ndevs), out_shape=jax.Sha...]
    convert_element_type x0 -> x1, other arithmetic: none -> 1.58 us  [local(): return finish(o, lse, placement, w_out, ndevs, slot_rows).astype(BF)]
    unnamed x1 -> x0, local copies, waits for them, and re-layouts: 1.52 us -> none
where the time goes in v5:
time: 87.3 us; the launch traced here: 87 us
  Pallas kernels  83.9 us (96%)
  other arithmetic  1.58 us (2%)
  local copies, waits for them, and re-layouts  1.54 us (2%)
    pallas_call x1, Pallas kernels, project(): pl.pallas_call(functools.partial(project_kernel, ndevs), out_shape=jax.Sh...  35.3 us
    pallas_call x1, Pallas kernels, finish(): pl.pallas_call(functools.partial(finish_kernel, ndevs), out_shape=jax.Sha...  32.6 us
    pallas_call x1, Pallas kernels, flash(): pl.pallas_call(functools.partial(flash_kernel, hl), out_shape=(jax.ShapeD...  16 us

profile of v5, /device:TPU:0, one launch (start us, length us, event | category | flops | bytes accessed | tf_op | source)
XLA Modules:
  0.0 87.0 jit_solution(12928542118684087171)
XLA Ops:
  0.0 35.3 %project.1.both_ref = bf16[16,272,128]{2,1,0:T(8,128)(2,1)} custom-call(bf16[2,2,8192]{2,1,0:T(2,128)(2,1)} %hidden_ref.1, bf16[8192,512]{1,0:T(8,128)(2,1)} %wq_ref.1, bf16[32,8192]{1,0:T(8,128)(2,1)} %bitcast.3), custom_call_target="tpu_custom_call" | custom-call | tf_op jit(solution)/shard_map/project/pallas_call | solution.py:265
  35.3 0.8 dynamic-slice_bitcast_fusion
  36.2 0.7 reshape.3.fresh_ref
  36.9 16.0 %flash.1 = (bf16[16,256,128]{2,1,0:T(8,128)(2,1)}, f32[16,16,128]{2,1,0:T(8,128)}) custom-call(s32[16]{0:T(128)} %lengths_ref.1, bf16[16,272,128]{2,1,0:T(8,128)(2,1)} %project.1.both_ref, bf16[4,512]{1,0:T(4,128)(2,1)} %reshape.3.fresh_ref, bf16[16,1024,512]{2,1,0:T(8,128)(2,1)} %cache_ref.1, bf16[256,1024]{1,0:T(8,128)(2,1)} %upk_ref.1, ...), custom_call_target="tpu_custom_call" | custom-call | flops 6442450944 | bytes 16777216 | tf_op jit(solution)/shard_map/flash/pallas_call | solution.py:107
  52.9 32.6 %finish.1 = f32[2,2,8192]{2,1,0:T(2,128)} custom-call(bf16[16,256,128]{2,1,0:T(8,128)(2,1)} %get-tuple-element.7.o_ref, f32[16,16,128]{2,1,0:T(8,128)} %get-tuple-element.8.l_ref, s32[16]{0:T(128)} %place_ref.1, bf16[512,8192]{1,0:T(8,128)(2,1)} %wo_ref.1), custom_call_target="tpu_custom_call" | custom-call | tf_op jit(solution)/shard_map/finish/pallas_call | solution.py:466
  85.5 1.6 %convert_element_type.3 = bf16[2,2,8192]{2,1,0:T(2,128)(2,1)} convert(f32[2,2,8192]{2,1,0:T(2,128)} %finish.1) | non-fusion elementwise | flops 32768 | bytes 196608 | tf_op jit(solution)/shard_map/convert_element_type | solution.py:500
  (1 shorter events, 0.0 us)
